TPU v7x, 512 devices: a whole 4x8x8 slice. The times are simulated.
512 devices in a mesh: grp: 8 (over z), dev: 64 (over y, x, core).
Axes of the slice: x: 4, y: 8, z: 8, core: 2. Of those that a mesh axis runs over, the one named last changes fastest.
Arguments:
- right_side: float32 [128, 2048, 128], P('grp', 'dev'), may hold values from -6 to 6
- coefficient: float32 [128, 2048, 128], P('grp', 'dev'), may hold values from 0.1 to 1
- solute: float32 [128, 2048, 128], P('grp', 'dev'), may hold values from 0.2 to 1.5
- diffusivity: float32 [128, 2048, 128], P('grp', 'dev'), may hold values from 0.05 to 0.5
- interface_flags: int32 [16, 256, 16], P('grp', 'dev'), may hold values 0 or 1
- coarse_inverse: float32 [512, 512], P(('grp', 'dev')), as said below
Outputs:
- pressure: float32 [128, 2048, 128], P('grp', 'dev')
- residual: float32 [128, 2048, 128], P('grp', 'dev')
- solute_image: float32 [128, 2048, 128], P('grp', 'dev')
Inputs may be any that keep to these rules, and one draw needn't show every extreme that they name: `coarse_inverse`: symmetric and positive definite; entries off the diagonal are nonnegative.
All inputs are finite; a program needn't handle non-finite values. No bound on the sum of `interface_flags` on one device may be relied on, other than what follows from the above.
Results may differ from a plain program's by a relative error of at most 0.003.
Values sent between devices are 32-bit elements; how exact they have to be, the bound alone decides.
A program may use at most 64 MiB of HBM per device.

v0:
```python
import math

import jax
import jax.numpy as jnp
import numpy as np
from jax import lax
from jax.sharding import PartitionSpec as P

ITERS = 2


HIGHEST = lax.Precision.HIGHEST
GLL_POINTS = [
    -1.0,
    -0.8717401485096066,
    -0.5917001814331423,
    -0.2092992179024789,
    0.2092992179024789,
    0.5917001814331423,
    0.8717401485096066,
    1.0,
]
GLL_WEIGHTS = [
    0.0357142857142857,
    0.2107042271435061,
    0.3411226924835044,
    0.4124587946587038,
    0.4124587946587038,
    0.3411226924835044,
    0.2107042271435061,
    0.0357142857142857,
]
SHIFT_MASS = 0.5
MASS_RATE = 2.0
GROWTH = 40.0
SEGREGATION = 0.7


def padded_2(x, sides, width):
    for axis, dim in sides:
        size, length = (lax.axis_size(axis), x.shape[dim])
        up = [(i, (i + 1) % size) for i in range(size - 1)]
        down = [(j, i) for i, j in up]
        last = lax.slice_in_dim(x, length - width, length, axis=dim)
        first = lax.slice_in_dim(x, 0, width, axis=dim)
        before = lax.ppermute(last, axis, up)
        after = lax.ppermute(first, axis, down)
        x = jnp.concatenate([before, x, after], axis=dim)
    return x


def derivative_table():
    products = []
    for row_at in range(8):
        value = 1.0
        for other in range(8):
            if other != row_at:
                value = value * (GLL_POINTS[row_at] - GLL_POINTS[other])
        products.append(value)
    table = [[0.0] * 8 for row_at in range(8)]
    for row_at in range(8):
        total = 0.0
        for other in range(8):
            if other != row_at:
                entry = (
                    products[row_at] / products[other] / (GLL_POINTS[row_at] - GLL_POINTS[other])
                )
                table[row_at][other] = entry
                total = total + entry
        table[row_at][row_at] = -total
    return np.array(table)


def margin_matrices():
    deriv_np = derivative_table()
    spacing = GLL_POINTS[1] - GLL_POINTS[0]
    stiffness = [[0.0] * 10 for row_at in range(10)]
    masses = [0.0] * 10
    for row_at in range(8):
        masses[row_at + 1] = GLL_WEIGHTS[row_at]
        for other in range(8):
            total = 0.0
            for point in range(8):
                total = (
                    total + deriv_np[point, row_at] * GLL_WEIGHTS[point] * deriv_np[point, other]
                )
            stiffness[row_at + 1][other + 1] = total
    for outer_end, inner_end in ((0, 1), (9, 8)):
        stiffness[outer_end][outer_end] += 1.0 / spacing
        stiffness[inner_end][inner_end] += 1.0 / spacing
        stiffness[outer_end][inner_end] -= 1.0 / spacing
        stiffness[inner_end][outer_end] -= 1.0 / spacing
        masses[outer_end] += 0.5 * spacing
        masses[inner_end] += 0.5 * spacing
    return (stiffness, masses)


def jacobi_eigen(matrix_rows):
    count_in = len(matrix_rows)
    work = [list(row_now) for row_now in matrix_rows]
    vectors = [
        [1.0 if other == row_at else 0.0 for other in range(count_in)] for row_at in range(count_in)
    ]
    for sweep in range(15):
        for first in range(count_in):
            for second in range(first + 1, count_in):
                entry = work[first][second]
                if entry != 0.0:
                    theta = (work[second][second] - work[first][first]) / (2.0 * entry)
                    sign_now = 1.0 if theta >= 0.0 else -1.0
                    tangent = sign_now / (abs(theta) + math.sqrt(theta * theta + 1.0))
                    cosine = 1.0 / math.sqrt(tangent * tangent + 1.0)
                    sine = tangent * cosine
                    for index in range(count_in):
                        left_val = work[index][first]
                        right_val = work[index][second]
                        work[index][first] = cosine * left_val - sine * right_val
                        work[index][second] = sine * left_val + cosine * right_val
                    for index in range(count_in):
                        left_val = work[first][index]
                        right_val = work[second][index]
                        work[first][index] = cosine * left_val - sine * right_val
                        work[second][index] = sine * left_val + cosine * right_val
                    for index in range(count_in):
                        left_val = vectors[index][first]
                        right_val = vectors[index][second]
                        vectors[index][first] = cosine * left_val - sine * right_val
                        vectors[index][second] = sine * left_val + cosine * right_val
    return ([work[index][index] for index in range(10 if count_in == 10 else count_in)], vectors)


def fdm_tables():
    stiffness, masses = margin_matrices()
    scaled = [
        [
            stiffness[row_at][other] / math.sqrt(masses[row_at] * masses[other])
            for other in range(10)
        ]
        for row_at in range(10)
    ]
    values, vectors = jacobi_eigen(scaled)
    basis = np.array(
        [
            [vectors[row_at][other] / math.sqrt(masses[row_at]) for other in range(10)]
            for row_at in range(10)
        ]
    )
    return (basis, np.array(values))


def z_forward_table(elements):
    basis, values = fdm_tables()
    extend_np = np.zeros((8 * elements, 10 * elements))
    for element in range(elements):
        for slot_in in range(10):
            source = 8 * element + slot_in - 1
            if slot_in == 0:
                source = 8 * element - 2
            if slot_in == 9:
                source = 8 * element + 9
            if 0 <= source < 8 * elements:
                extend_np[source, 10 * element + slot_in] = 1.0
    return extend_np @ np.kron(np.eye(elements), basis)


def z_backward_table(elements):
    basis, values = fdm_tables()
    return np.kron(np.eye(elements), basis[1:9].T)


def eigen_sums(count_x, count_y, count_z):
    basis, values = fdm_tables()
    first_vec = jnp.asarray(np.tile(values, count_x), jnp.float32)
    second_vec = jnp.asarray(np.tile(values, count_y), jnp.float32)
    third_vec = jnp.asarray(np.tile(values, count_z), jnp.float32)
    return (
        first_vec[:, None, None] + second_vec[None, :, None] + third_vec[None, None, :] + SHIFT_MASS
    )


def z_derivative(elements):
    return np.kron(np.eye(elements), derivative_table().T)


def z_pairs(elements):
    pairs_np = np.eye(8 * elements)
    for element in range(elements - 1):
        pairs_np[8 * element + 7, 8 * element + 8] = 1.0
        pairs_np[8 * element + 8, 8 * element + 7] = 1.0
    return pairs_np


def axis_factors(start_at, count_in, total_len):
    positions = start_at + jnp.arange(count_in, dtype=jnp.int32)
    inside = (positions > 0) & (positions < total_len - 1)
    remainder = positions % 8
    shared = ((remainder == 0) | (remainder == 7)) & inside
    keep_part = jnp.where(inside, 1.0, 0.0).astype(jnp.float32)
    share_part = jnp.where(shared, 0.5, 1.0).astype(jnp.float32)
    return (keep_part, share_part)


def outer_three(first_vec, second_vec, third_vec):
    return first_vec[:, None, None] * second_vec[None, :, None] * third_vec[None, None, :]


def tiled_weights(count_in):
    return jnp.asarray(np.tile(np.array(GLL_WEIGHTS), count_in // 8), jnp.float32)


def pair_sum(inner_part, low_plane, high_plane, along_dim):
    length_along = inner_part.shape[along_dim]
    number = length_along // 8
    firsts = lax.slice_in_dim(inner_part, 0, length_along, 8, along_dim)
    last_planes = lax.slice_in_dim(inner_part, 7, length_along, 8, along_dim)
    next_first = jnp.concatenate(
        [lax.slice_in_dim(firsts, 1, number, 1, along_dim), high_plane], along_dim
    )
    prev_last = jnp.concatenate(
        [low_plane, lax.slice_in_dim(last_planes, 0, number - 1, 1, along_dim)], along_dim
    )
    split_shape = inner_part.shape[:along_dim] + (number, 8) + inner_part.shape[along_dim + 1 :]
    single_shape = inner_part.shape[:along_dim] + (number, 1) + inner_part.shape[along_dim + 1 :]
    middle = lax.slice_in_dim(inner_part.reshape(split_shape), 1, 7, 1, along_dim + 1)
    joined = jnp.concatenate(
        [
            (firsts + prev_last).reshape(single_shape),
            middle,
            (last_planes + next_first).reshape(single_shape),
        ],
        along_dim + 1,
    )
    return joined.reshape(inner_part.shape)


def stiffness_apply(values_in, coeff_in, derivative, z_forward, z_backward, weight_cube):
    size_x, size_y, size_z = values_in.shape
    block_shape = (size_x // 8, 8, size_y // 8, 8, size_z)
    blocks = values_in.reshape(block_shape)
    grad_x = jnp.einsum("pi,aibjz->apbjz", derivative, blocks, precision=HIGHEST).reshape(
        values_in.shape
    )
    grad_y = jnp.einsum("qj,aibjz->aibqz", derivative, blocks, precision=HIGHEST).reshape(
        values_in.shape
    )
    grad_z = jnp.dot(values_in, z_forward, precision=HIGHEST)
    scaled = coeff_in * weight_cube
    back_x = jnp.einsum(
        "pi,apbjz->aibjz", derivative, (scaled * grad_x).reshape(block_shape), precision=HIGHEST
    )
    back_y = jnp.einsum(
        "qj,aibqz->aibjz", derivative, (scaled * grad_y).reshape(block_shape), precision=HIGHEST
    )
    back_z = jnp.dot(scaled * grad_z, z_backward, precision=HIGHEST)
    return back_x.reshape(values_in.shape) + back_y.reshape(values_in.shape) + back_z


def element_apply(values_in, along_dim, table_rows):
    width = table_rows.shape[1]
    number = values_in.shape[along_dim] // width
    split_shape = values_in.shape[:along_dim] + (number, width) + values_in.shape[along_dim + 1 :]
    blocks = values_in.reshape(split_shape)
    if along_dim == 0:
        solved = jnp.einsum("pi,aiyz->apyz", table_rows, blocks, precision=HIGHEST)
    else:
        solved = jnp.einsum("pi,xaiz->xapz", table_rows, blocks, precision=HIGHEST)
    final_shape = (
        values_in.shape[:along_dim]
        + (table_rows.shape[0] * number,)
        + values_in.shape[along_dim + 1 :]
    )
    return solved.reshape(final_shape)


def extend_solve(padded, along_dim, table_rows):
    length_pad = padded.shape[along_dim]
    number = (length_pad - 4) // 8
    split_shape = padded.shape[:along_dim] + (number, 8) + padded.shape[along_dim + 1 :]
    single_shape = padded.shape[:along_dim] + (number, 1) + padded.shape[along_dim + 1 :]
    inner_part = lax.slice_in_dim(padded, 2, length_pad - 2, 1, along_dim).reshape(split_shape)
    low_plane = lax.slice_in_dim(padded, 0, 8 * number, 8, along_dim).reshape(single_shape)
    high_plane = lax.slice_in_dim(padded, 11, length_pad, 8, along_dim).reshape(single_shape)
    extended = jnp.concatenate([low_plane, inner_part, high_plane], along_dim + 1)
    final_shape = padded.shape[:along_dim] + (10 * number,) + padded.shape[along_dim + 1 :]
    return element_apply(extended.reshape(final_shape), along_dim, table_rows)


def schwarz_apply(padded, z_fore, z_back, forward_rows, back_rows):
    along_z = jnp.dot(padded, z_fore, precision=HIGHEST)
    into_x = extend_solve(along_z, 0, forward_rows)
    into_y = extend_solve(into_x, 1, forward_rows)
    denom = eigen_sums(into_y.shape[0] // 10, into_y.shape[1] // 10, into_y.shape[2] // 10)
    divided = into_y / denom
    back_x = element_apply(divided, 0, back_rows)
    back_y = element_apply(back_x, 1, back_rows)
    return jnp.dot(back_y, z_back, precision=HIGHEST)


def shards(right_side, coefficient, solute, diffusivity, interface_flags, coarse_inverse):
    size_x, size_y, size_z = right_side.shape
    elements_z = size_z // 8
    derivative = jnp.asarray(derivative_table(), jnp.float32)
    z_forward = jnp.asarray(z_derivative(elements_z), jnp.float32)
    z_backward = jnp.asarray(z_derivative(elements_z).T, jnp.float32)
    z_sum = jnp.asarray(z_pairs(elements_z), jnp.float32)
    z_fore = jnp.asarray(z_forward_table(elements_z), jnp.float32)
    z_back = jnp.asarray(z_backward_table(elements_z), jnp.float32)
    basis, values = fdm_tables()
    forward_rows = jnp.asarray(basis.T, jnp.float32)
    back_rows = jnp.asarray(basis[1:9], jnp.float32)
    weight_x = tiled_weights(size_x)
    weight_y = tiled_weights(size_y)
    weight_z = tiled_weights(size_z)
    weight_cube = outer_three(weight_x, weight_y, weight_z)
    keep_x, share_x = axis_factors(
        lax.axis_index("grp") * size_x, size_x, size_x * lax.axis_size("grp")
    )
    keep_y, share_y = axis_factors(
        lax.axis_index("dev") * size_y, size_y, size_y * lax.axis_size("dev")
    )
    keep_z, share_z = axis_factors(0, size_z, size_z)
    dirichlet_mask = outer_three(keep_x, keep_y, keep_z)
    inv_mult = outer_three(share_x, share_y, share_z)
    q_scale = 1.0 / math.sqrt(size_x * size_y * size_z)
    coarse_row = coarse_inverse[0]

    def assemble(values_in):
        padded = padded_2(values_in, (("grp", 0), ("dev", 1)), 1)
        along_x = pair_sum(padded[1:-1], padded[0:1], padded[-1:], 0)
        along_y = pair_sum(along_x[:, 1:-1], along_x[:, 0:1], along_x[:, -1:], 1)
        return jnp.dot(along_y, z_sum, precision=HIGHEST)

    def local_coarse(values_in):
        return jnp.sum(values_in * inv_mult) * q_scale

    def coarse_gathered(q_value):
        everything = lax.all_gather(q_value.reshape(1), ("grp", "dev"), axis=0, tiled=True)
        return jnp.dot(coarse_row, everything, precision=HIGHEST)

    def precondition(residual_now, coarse_value):
        padded = padded_2(residual_now, (("grp", 0), ("dev", 1)), 2)
        solved = schwarz_apply(padded, z_fore, z_back, forward_rows, back_rows)
        return assemble(solved + coarse_value) * inv_mult * dirichlet_mask

    def energy_sum(first_field, second_field):
        return lax.psum(jnp.sum(first_field * second_field * inv_mult), ("grp", "dev"))

    start_vec = assemble(right_side) * dirichlet_mask
    pressure = jnp.zeros_like(right_side)
    residual = start_vec
    precond_now = precondition(residual, coarse_gathered(local_coarse(residual)))
    energy_now = energy_sum(residual, precond_now)
    direction = precond_now
    coarse_value = jnp.zeros((), jnp.float32)
    for step_index in range(ITERS):
        applied = (
            assemble(
                stiffness_apply(
                    direction, coefficient, derivative, z_forward, z_backward, weight_cube
                )
            )
            * dirichlet_mask
        )
        local_curve = jnp.sum(direction * applied * inv_mult)
        step_length = energy_now / lax.psum(local_curve, ("grp", "dev"))
        pressure = pressure + step_length * direction
        residual = residual - step_length * applied
        if step_index + 1 < ITERS:
            coarse_value = coarse_gathered(local_coarse(residual))
            precond_now = precondition(residual, coarse_value)
            energy_next = energy_sum(residual, precond_now)
            direction = precond_now + energy_next / energy_now * direction
            energy_now = energy_next
    flag_points = jnp.repeat(
        jnp.repeat(jnp.repeat(interface_flags, 8, axis=0), 8, axis=1), 8, axis=2
    ).astype(jnp.float32)
    bottom = jnp.where(jnp.arange(size_z, dtype=jnp.int32) % 8 == 0, 1.0, 0.0).astype(jnp.float32)
    face_weight = outer_three(weight_x, weight_y, bottom)
    flux = GROWTH * SEGREGATION * flag_points * face_weight * solute
    local_image = (
        stiffness_apply(solute, diffusivity, derivative, z_forward, z_backward, weight_cube)
        + MASS_RATE * weight_cube * solute
        + flux
    )
    solute_image = assemble(local_image)
    return (pressure, residual, solute_image)


def solution(mesh):
    placed = (
        P("grp", "dev", None),
        P("grp", "dev", None),
        P("grp", "dev", None),
        P("grp", "dev", None),
        P("grp", "dev", None),
        P(("grp", "dev"), None),
    )
    return jax.shard_map(
        shards,
        mesh=mesh,
        in_specs=placed,
        out_specs=(P("grp", "dev", None), P("grp", "dev", None), P("grp", "dev", None)),
        check_vma=False,
    )
```

profile of v0, /device:TPU:1, one launch (start us, length us, event | category | flops | bytes accessed | tf_op | source)
XLA Modules:
  0.0 681.2 jit_solution(15535396559702392199)
XLA Ops:
  1.4 4.8 collective-permute-start
  9.4 1.9 collective-permute-done.1
  11.3 5.8 collective-permute-start.3
  17.1 1.9 collective-permute-start.2
  23.5 4.0 collective-permute-start.4
  28.3 104.6 %all-reduce = f32[512]{0:T(512)S(1)} all-reduce(f32[512]{0:T(512)S(1)} %dynamic-update-slice), channel_id=1, replica_groups=mesh['grp'=8,'dev'=64] {'grp','dev'}, use_global_device_ids=true, to_apply=%add | all-reduce | flops 512 | bytes 4096
  132.9 2.6 collective-permute-start.7
  135.5 3.6 collective-permute-start.6
  144.0 1.6 convolution_bitcast_fusion.1
  152.1 4.0 collective-permute-start.8
  157.0 1.9 collective-permute-start.11
  158.9 5.8 collective-permute-start.10
  170.6 4.5 collective-permute-start.12
  176.0 1.9 collective-permute-start.15
  177.9 5.0 collective-permute-start.14
  186.0 108.9 %all-reduce.2 = (f32[]{:T(128)}, f32[]{:T(128)}) all-reduce(f32[]{:T(128)} %get-tuple-element.4, f32[]{:T(128)} %get-tuple-element.3), channel_id=1, replica_groups=mesh['grp'=8,'dev'=64] {'grp','dev'}, use_global_device_ids=true, to_apply=%region_2.3 | all-reduce | flops 2 | bytes 16 | tf_op jit(solution)/shard_map/psum | solution.py:346
  298.2 4.0 collective-permute-start.16
  304.2 96.3 %all-reduce.1 = f32[512]{0:T(512)S(1)} all-reduce(f32[512]{0:T(512)S(1)} %dynamic-update-slice.1), channel_id=1, replica_groups=mesh['grp'=8,'dev'=64] {'grp','dev'}, use_global_device_ids=true, to_apply=%add.1 | all-reduce | flops 512 | bytes 4096
  400.5 2.6 collective-permute-start.19
  403.1 3.2 collective-permute-start.18
  411.8 2.7 convolution_bitcast_fusion
  422.0 4.0 collective-permute-start.20
  426.9 2.4 collective-permute-start.23
  429.4 4.8 collective-permute-start.22
  437.2 104.7 %psum.30 = f32[]{:T(128)} all-reduce(f32[]{:T(128)} %get-tuple-element.104), channel_id=1, replica_groups=mesh['grp'=8,'dev'=64] {'grp','dev'}, use_global_device_ids=true, to_apply=%region_7.8 | all-reduce | flops 1 | bytes 8 | tf_op jit(solution)/shard_map/psum | solution.py:346
  547.6 4.0 collective-permute-start.24
  554.4 4.0 collective-permute-start.28
  558.4 3.7 collective-permute-start.27
  562.1 3.6 collective-permute-start.26
  565.7 1.9 collective-permute-start.31
  567.6 3.6 collective-permute-start.30
  573.9 103.1 %psum.31 = f32[]{:T(128)} all-reduce(f32[]{:T(128)} %get-tuple-element.106), channel_id=1, replica_groups=mesh['grp'=8,'dev'=64] {'grp','dev'}, use_global_device_ids=true, to_apply=%region_9.10 | all-reduce | flops 1 | bytes 8 | tf_op jit(solution)/shard_map/psum | solution.py:365
  (333 shorter events, 61.7 us)
Async XLA Ops:
  1.4 7.1 %collective-permute-start = (f32[1,32,128]{2,1,0:T(8,128)S(1)}, f32[1,32,128]{2,1,0:T(8,128)S(1)}, u32[]{:S(2)}, u32[]{:S(2)}) collective-permute-start(f32[1,32,128]{2,1,0:T(8,128)S(1)} %get-tuple-element.98), channel_id=1, source_target_pairs={{0,64},{64,128},{128,192},{192,256},{256,320},{320,384},{384,448},... | collective-permute-start | bytes 49160 | tf_op jit(solution)/shard_map/ppermute | solution.py:46
  6.2 5.1 collective-permute-start.1
  11.3 7.7 %collective-permute-start.3 = (f32[18,1,128]{2,1,0:T(1,128)S(1)}, f32[18,1,128]{2,1,0:T(1,128)S(1)}, u32[]{:S(2)}, u32[]{:S(2)}) collective-permute-start(f32[18,1,128]{2,1,0:T(1,128)S(1)} %get-tuple-element.76), channel_id=1, source_target_pairs={{1,0},{2,1},{3,2},{4,3},{5,4},{6,5},{7,6},{8,7},{9,8},{10,9},{11,1... | collective-permute-start | bytes 27656 | tf_op jit(solution)/shard_map/ppermute | solution.py:47
  17.1 3.1 collective-permute-start.2
  22.2 110.7 %collective-permute-start.5 = (f32[2,32,128]{2,1,0:T(8,128)S(1)}, f32[2,32,128]{2,1,0:T(8,128)S(1)}, u32[]{:S(2)}, u32[]{:S(2)}) collective-permute-start(f32[2,32,128]{2,1,0:T(8,128)S(1)} %get-tuple-element.96), channel_id=1, source_target_pairs={{64,0},{128,64},{192,128},{256,192},{320,256},{384,320},{448,384},... | collective-permute-start | bytes 98312 | tf_op jit(solution)/shard_map/ppermute | solution.py:47
  23.5 109.4 %collective-permute-start.4 = (f32[2,32,128]{2,1,0:T(8,128)S(1)}, f32[2,32,128]{2,1,0:T(8,128)S(1)}, u32[]{:S(2)}, u32[]{:S(2)}) collective-permute-start(f32[2,32,128]{2,1,0:T(8,128)S(1)} %get-tuple-element.95), channel_id=1, source_target_pairs={{0,64},{64,128},{128,192},{192,256},{256,320},{320,384},{384,448},... | collective-permute-start | bytes 98312 | tf_op jit(solution)/shard_map/ppermute | solution.py:46
  132.9 6.8 collective-permute-start.7
  135.5 4.5 collective-permute-start.6
  150.8 5.3 collective-permute-start.9
  152.1 4.8 collective-permute-start.8
  157.0 8.0 %collective-permute-start.11 = (f32[18,1,128]{2,1,0:T(1,128)S(1)}, f32[18,1,128]{2,1,0:T(1,128)S(1)}, u32[]{:S(2)}, u32[]{:S(2)}) collective-permute-start(f32[18,1,128]{2,1,0:T(1,128)S(1)} %get-tuple-element.74), channel_id=1, source_target_pairs={{1,0},{2,1},{3,2},{4,3},{5,4},{6,5},{7,6},{8,7},{9,8},{10,9},{11,1... | collective-permute-start | bytes 27656 | tf_op jit(solution)/shard_map/ppermute | solution.py:47
  158.9 6.1 collective-permute-start.10
  169.3 6.0 collective-permute-start.13
  170.6 5.4 collective-permute-start.12
  176.0 8.1 %collective-permute-start.15 = (f32[18,1,128]{2,1,0:T(1,128)S(1)}, f32[18,1,128]{2,1,0:T(1,128)S(1)}, u32[]{:S(2)}, u32[]{:S(2)}) collective-permute-start(f32[18,1,128]{2,1,0:T(1,128)S(1)} %get-tuple-element.72), channel_id=1, source_target_pairs={{1,0},{2,1},{3,2},{4,3},{5,4},{6,5},{7,6},{8,7},{9,8},{10,9},{11,1... | collective-permute-start | bytes 27656 | tf_op jit(solution)/shard_map/ppermute | solution.py:47
  177.9 6.2 collective-permute-start.14
  296.9 103.5 %collective-permute-start.17 = (f32[2,32,128]{2,1,0:T(8,128)S(1)}, f32[2,32,128]{2,1,0:T(8,128)S(1)}, u32[]{:S(2)}, u32[]{:S(2)}) collective-permute-start(f32[2,32,128]{2,1,0:T(8,128)S(1)} %get-tuple-element.90), channel_id=1, source_target_pairs={{64,0},{128,64},{192,128},{256,192},{320,256},{384,320},{448,384},... | collective-permute-start | bytes 98312 | tf_op jit(solution)/shard_map/ppermute | solution.py:47
  298.2 102.2 %collective-permute-start.16 = (f32[2,32,128]{2,1,0:T(8,128)S(1)}, f32[2,32,128]{2,1,0:T(8,128)S(1)}, u32[]{:S(2)}, u32[]{:S(2)}) collective-permute-start(f32[2,32,128]{2,1,0:T(8,128)S(1)} %get-tuple-element.89), channel_id=1, source_target_pairs={{0,64},{64,128},{128,192},{192,256},{256,320},{320,384},{384,448},... | collective-permute-start | bytes 98312 | tf_op jit(solution)/shard_map/ppermute | solution.py:46
  400.5 6.4 collective-permute-start.19
  403.1 3.9 collective-permute-start.18
  420.7 5.7 collective-permute-start.21
  422.0 4.9 collective-permute-start.20
  426.9 8.4 %collective-permute-start.23 = (f32[18,1,128]{2,1,0:T(1,128)S(1)}, f32[18,1,128]{2,1,0:T(1,128)S(1)}, u32[]{:S(2)}, u32[]{:S(2)}) collective-permute-start(f32[18,1,128]{2,1,0:T(1,128)S(1)} %get-tuple-element.70), channel_id=1, source_target_pairs={{1,0},{2,1},{3,2},{4,3},{5,4},{6,5},{7,6},{8,7},{9,8},{10,9},{11,1... | collective-permute-start | bytes 27656 | tf_op jit(solution)/shard_map/ppermute | solution.py:47
  429.4 5.9 collective-permute-start.22
  546.3 12.1 %collective-permute-start.25 = (f32[1,32,128]{2,1,0:T(8,128)S(1)}, f32[1,32,128]{2,1,0:T(8,128)S(1)}, u32[]{:S(2)}, u32[]{:S(2)}) collective-permute-start(f32[1,32,128]{2,1,0:T(8,128)S(1)} %get-tuple-element.86), channel_id=1, source_target_pairs={{64,0},{128,64},{192,128},{256,192},{320,256},{384,320},{448,384},... | collective-permute-start | bytes 49160 | tf_op jit(solution)/shard_map/ppermute | solution.py:47
  547.6 10.8 %collective-permute-start.24 = (f32[1,32,128]{2,1,0:T(8,128)S(1)}, f32[1,32,128]{2,1,0:T(8,128)S(1)}, u32[]{:S(2)}, u32[]{:S(2)}) collective-permute-start(f32[1,32,128]{2,1,0:T(8,128)S(1)} %get-tuple-element.85), channel_id=1, source_target_pairs={{0,64},{64,128},{128,192},{192,256},{256,320},{320,384},{384,448},... | collective-permute-start | bytes 49160 | tf_op jit(solution)/shard_map/ppermute | solution.py:46
  553.1 12.6 %collective-permute-start.29 = (f32[1,32,128]{2,1,0:T(8,128)S(1)}, f32[1,32,128]{2,1,0:T(8,128)S(1)}, u32[]{:S(2)}, u32[]{:S(2)}) collective-permute-start(f32[1,32,128]{2,1,0:T(8,128)S(1)} %get-tuple-element.84), channel_id=1, source_target_pairs={{64,0},{128,64},{192,128},{256,192},{320,256},{384,320},{448,384},... | collective-permute-start | bytes 49160 | tf_op jit(solution)/shard_map/ppermute | solution.py:47
  554.4 11.3 %collective-permute-start.28 = (f32[1,32,128]{2,1,0:T(8,128)S(1)}, f32[1,32,128]{2,1,0:T(8,128)S(1)}, u32[]{:S(2)}, u32[]{:S(2)}) collective-permute-start(f32[1,32,128]{2,1,0:T(8,128)S(1)} %get-tuple-element.83), channel_id=1, source_target_pairs={{0,64},{64,128},{128,192},{192,256},{256,320},{320,384},{384,448},... | collective-permute-start | bytes 49160 | tf_op jit(solution)/shard_map/ppermute | solution.py:46
  558.4 12.9 %collective-permute-start.27 = (f32[18,1,128]{2,1,0:T(1,128)S(1)}, f32[18,1,128]{2,1,0:T(1,128)S(1)}, u32[]{:S(2)}, u32[]{:S(2)}) collective-permute-start(f32[18,1,128]{2,1,0:T(1,128)S(1)} %get-tuple-element.68), channel_id=1, source_target_pairs={{1,0},{2,1},{3,2},{4,3},{5,4},{6,5},{7,6},{8,7},{9,8},{10,9},{11,1... | collective-permute-start | bytes 27656 | tf_op jit(solution)/shard_map/ppermute | solution.py:47
  562.1 9.2 %collective-permute-start.26 = (f32[18,1,128]{2,1,0:T(1,128)S(1)}, f32[18,1,128]{2,1,0:T(1,128)S(1)}, u32[]{:S(2)}, u32[]{:S(2)}) collective-permute-start(f32[18,1,128]{2,1,0:T(1,128)S(1)} %get-tuple-element.67), channel_id=1, source_target_pairs={{0,1},{1,2},{2,3},{3,4},{4,5},{5,6},{6,7},{7,8},{8,9},{9,10},{10,1... | collective-permute-start | bytes 27656 | tf_op jit(solution)/shard_map/ppermute | solution.py:46
  565.7 6.0 collective-permute-start.31
  567.6 4.4 collective-permute-start.30
  (43 other events, 1302.6 us)
where the time goes:
time: 691 us; the launch traced here: 681 us
  blocking collectives  517 us (75%)
  starting transfers between devices  97.9 us (14%)
  matrix products  31 us (4%)
  local copies, waits for them, and re-layouts  13.4 us (2%)
  between operations  8.28 us (1%)
  other arithmetic  7.43 us (1%)
    psum x2, blocking collectives, energy_sum(): lax.psum(jnp.sum(first_field * second_field * inv_mult), ('grp', 'dev'))  214 us
    unnamed x2, blocking collectives  201 us
    psum x1, blocking collectives, shards(): step_length = energy_now / lax.psum(local_curve, ('grp', 'dev'))  103 us
    ppermute x16, starting transfers between devices, padded_2(): before = lax.ppermute(last, axis, up)  64.8 us
    ppermute x16, starting transfers between devices, padded_2(): after = lax.ppermute(first, axis, down)  33.1 us
  transfers between devices with their start and end apart: 32, of which 8 were waited for; matrix products, arithmetic and copies ran while one was open for 1% of the time, Pallas kernels for 0%

commit v1 on v0

v1 whole, which is shorter than its diff:
```python
import functools
import math

import jax
import jax.numpy as jnp
import ml_dtypes
import numpy as np
from jax import lax
from jax.experimental import pallas as pl
from jax.experimental.pallas import tpu as pltpu
from jax.sharding import PartitionSpec as P

GLL_POINTS = [
    -1.0,
    -0.8717401485096066,
    -0.5917001814331423,
    -0.2092992179024789,
    0.2092992179024789,
    0.5917001814331423,
    0.8717401485096066,
    1.0,
]
GLL_WEIGHTS = [
    0.0357142857142857,
    0.2107042271435061,
    0.3411226924835044,
    0.4124587946587038,
    0.4124587946587038,
    0.3411226924835044,
    0.2107042271435061,
    0.0357142857142857,
]
SHIFT_MASS = 0.5
MASS_RATE = 2.0
GROWTH = 40.0
SEGREGATION = 0.7


def derivative_table():
    products = []
    for row_at in range(8):
        value = 1.0
        for other in range(8):
            if other != row_at:
                value = value * (GLL_POINTS[row_at] - GLL_POINTS[other])
        products.append(value)
    table = [[0.0] * 8 for row_at in range(8)]
    for row_at in range(8):
        total = 0.0
        for other in range(8):
            if other != row_at:
                entry = (
                    products[row_at] / products[other] / (GLL_POINTS[row_at] - GLL_POINTS[other])
                )
                table[row_at][other] = entry
                total = total + entry
        table[row_at][row_at] = -total
    return np.array(table)


def margin_matrices():
    deriv_np = derivative_table()
    spacing = GLL_POINTS[1] - GLL_POINTS[0]
    stiffness = [[0.0] * 10 for row_at in range(10)]
    masses = [0.0] * 10
    for row_at in range(8):
        masses[row_at + 1] = GLL_WEIGHTS[row_at]
        for other in range(8):
            total = 0.0
            for point in range(8):
                total = (
                    total + deriv_np[point, row_at] * GLL_WEIGHTS[point] * deriv_np[point, other]
                )
            stiffness[row_at + 1][other + 1] = total
    for outer_end, inner_end in ((0, 1), (9, 8)):
        stiffness[outer_end][outer_end] += 1.0 / spacing
        stiffness[inner_end][inner_end] += 1.0 / spacing
        stiffness[outer_end][inner_end] -= 1.0 / spacing
        stiffness[inner_end][outer_end] -= 1.0 / spacing
        masses[outer_end] += 0.5 * spacing
        masses[inner_end] += 0.5 * spacing
    return (stiffness, masses)


def jacobi_eigen(matrix_rows):
    count_in = len(matrix_rows)
    work = [list(row_now) for row_now in matrix_rows]
    vectors = [
        [1.0 if other == row_at else 0.0 for other in range(count_in)] for row_at in range(count_in)
    ]
    for sweep in range(15):
        for first in range(count_in):
            for second in range(first + 1, count_in):
                entry = work[first][second]
                if entry != 0.0:
                    theta = (work[second][second] - work[first][first]) / (2.0 * entry)
                    sign_now = 1.0 if theta >= 0.0 else -1.0
                    tangent = sign_now / (abs(theta) + math.sqrt(theta * theta + 1.0))
                    cosine = 1.0 / math.sqrt(tangent * tangent + 1.0)
                    sine = tangent * cosine
                    for index in range(count_in):
                        left_val = work[index][first]
                        right_val = work[index][second]
                        work[index][first] = cosine * left_val - sine * right_val
                        work[index][second] = sine * left_val + cosine * right_val
                    for index in range(count_in):
                        left_val = work[first][index]
                        right_val = work[second][index]
                        work[first][index] = cosine * left_val - sine * right_val
                        work[second][index] = sine * left_val + cosine * right_val
                    for index in range(count_in):
                        left_val = vectors[index][first]
                        right_val = vectors[index][second]
                        vectors[index][first] = cosine * left_val - sine * right_val
                        vectors[index][second] = sine * left_val + cosine * right_val
    return ([work[index][index] for index in range(10 if count_in == 10 else count_in)], vectors)


def fdm_tables():
    stiffness, masses = margin_matrices()
    scaled = [
        [
            stiffness[row_at][other] / math.sqrt(masses[row_at] * masses[other])
            for other in range(10)
        ]
        for row_at in range(10)
    ]
    values, vectors = jacobi_eigen(scaled)
    basis = np.array(
        [
            [vectors[row_at][other] / math.sqrt(masses[row_at]) for other in range(10)]
            for row_at in range(10)
        ]
    )
    return (basis, np.array(values))


def z_forward_table(elements):
    basis, values = fdm_tables()
    extend_np = np.zeros((8 * elements, 10 * elements))
    for element in range(elements):
        for slot_in in range(10):
            source = 8 * element + slot_in - 1
            if slot_in == 0:
                source = 8 * element - 2
            if slot_in == 9:
                source = 8 * element + 9
            if 0 <= source < 8 * elements:
                extend_np[source, 10 * element + slot_in] = 1.0
    return extend_np @ np.kron(np.eye(elements), basis)


def z_backward_table(elements):
    basis, values = fdm_tables()
    return np.kron(np.eye(elements), basis[1:9].T)


def z_derivative(elements):
    return np.kron(np.eye(elements), derivative_table().T)


def z_pairs(elements):
    pairs_np = np.eye(8 * elements)
    for element in range(elements - 1):
        pairs_np[8 * element + 7, 8 * element + 8] = 1.0
        pairs_np[8 * element + 8, 8 * element + 7] = 1.0
    return pairs_np


LOCAL_X, LOCAL_Y, LOCAL_Z = (16, 32, 128)
ROWS = LOCAL_X * LOCAL_Y
DIRS = ((-1, 0), (1, 0), (0, -1), (0, 1), (-1, -1), (-1, 1), (1, -1), (1, 1))
F32 = jnp.float32
BF16 = jnp.bfloat16
MESH_ID = pl.DeviceIdType.MESH


def split_np(table):
    high = np.asarray(table, np.float32).astype(ml_dtypes.bfloat16)
    low = (np.asarray(table, np.float64) - high.astype(np.float64)).astype(ml_dtypes.bfloat16)
    return (high, low)


def left_table(matrix, rows):
    high, low = split_np(matrix)
    joined = np.concatenate([high, high, low], axis=1)
    out = np.zeros((rows, 128), ml_dtypes.bfloat16)
    out[: joined.shape[0], : joined.shape[1]] = joined
    return out


def y_pairs():
    pairs = np.eye(LOCAL_Y)
    for element in range(LOCAL_Y // 8 - 1):
        pairs[8 * element + 7, 8 * element + 8] = 1.0
        pairs[8 * element + 8, 8 * element + 7] = 1.0
    return pairs


def inner_share(count_in):
    share = np.ones(count_in)
    for position in range(count_in):
        if position % 8 in (0, 7) and position not in (0, count_in - 1):
            share[position] = 0.5
    return share


def padded_to(matrix, rows, columns):
    out = np.zeros((rows, columns))
    out[: matrix.shape[0], : matrix.shape[1]] = matrix
    return out


def make_tables():
    basis, values = fdm_tables()
    deriv = derivative_table()
    ends = np.ones(LOCAL_Z)
    ends[0] = 0.0
    ends[-1] = 0.0
    pairs_z = z_pairs(LOCAL_Z // 8)
    fore = pairs_z @ np.diag(ends) @ z_forward_table(LOCAL_Z // 8)
    back = z_backward_table(LOCAL_Z // 8) @ pairs_z @ np.diag(ends * inner_share(LOCAL_Z))
    fore_hi, fore_lo = split_np(padded_to(fore, 128, 256))
    back_hi, back_lo = split_np(padded_to(back, 256, 128))
    zf1 = np.concatenate([fore_hi, fore_hi], axis=0)
    zb1 = np.concatenate([back_hi, back_lo], axis=1)

    def square(matrix):
        high, low = split_np(matrix)
        return np.concatenate([np.concatenate([high, low], axis=1)] * 2, axis=0)

    deriv_z = np.kron(np.eye(LOCAL_Z // 8), deriv.T)
    deriv_y = np.kron(np.eye(LOCAL_Y // 8), deriv)
    count_y = LOCAL_Y // 8
    extend = np.zeros((10 * count_y, 40))
    for element in range(count_y):
        for slot in range(10):
            source = 8 * element + slot - 1
            if slot == 0:
                source = 8 * element - 2 if element else 32
            if slot == 9:
                source = 8 * element + 9 if element + 1 < count_y else 33
            extend[10 * element + slot, source] = 1.0
    y_fore = np.kron(np.eye(count_y), basis.T) @ extend
    y_back = np.diag(inner_share(LOCAL_Y)) @ y_pairs() @ np.kron(np.eye(count_y), basis[1:9])
    sums = (
        values[:, None, None]
        + np.tile(values, count_y)[None, :, None]
        + np.tile(values, LOCAL_Z // 8)[None, None, :]
        + SHIFT_MASS
    )
    recip = np.zeros((10 * 40, 256), np.float32)
    recip[:, :160] = (1.0 / sums).reshape(400, 160)
    weights = np.array(GLL_WEIGHTS)
    wyz = np.tile(weights, count_y)[:, None] * np.tile(weights, LOCAL_Z // 8)[None, :]
    spread = np.zeros((LOCAL_Z // 8, LOCAL_Z), ml_dtypes.bfloat16)
    for element in range(LOCAL_Z // 8):
        spread[element, 8 * element] = 1.0
    return dict(
        yf=left_table(y_fore, 48),
        yb=left_table(y_back, 32),
        yd=left_table(deriv_y, 32),
        ydt=left_table(deriv_y.T, 32),
        zf1=zf1,
        zf2=fore_lo,
        zb1=zb1,
        zd=square(deriv_z),
        zdt=square(deriv_z.T),
        wyz=wyz.astype(np.float32),
        spread=spread,
        recip=recip,
    )


TABLE_NAMES = ("yf", "yb", "yd", "ydt", "zf1", "zf2", "zb1", "zd", "zdt", "wyz", "spread", "recip")


def parity_signs(basis):
    signs = []
    for mode in range(10):
        even = np.abs(basis[:, mode] - basis[::-1, mode]).max()
        odd = np.abs(basis[:, mode] + basis[::-1, mode]).max()
        signs.append(1 if even < odd else -1)
    return signs


def weighted(coefficients, terms):
    total = None
    for coefficient, term in zip(coefficients, terms):
        piece = term * float(coefficient)
        total = piece if total is None else total + piece
    return total


def x_derive(values, matrix):
    sums = [values[i] + values[7 - i] for i in range(4)]
    gaps = [values[i] - values[7 - i] for i in range(4)]
    out = [None] * 8
    for p in range(4):
        first = weighted([(matrix[p, i] + matrix[p, 7 - i]) / 2 for i in range(4)], sums)
        second = weighted([(matrix[p, i] - matrix[p, 7 - i]) / 2 for i in range(4)], gaps)
        out[p] = second + first
        out[7 - p] = second - first
    return out


def x_modes(values, basis, signs):
    sums = [values[i] + values[9 - i] for i in range(5)]
    gaps = [values[i] - values[9 - i] for i in range(5)]
    return [
        weighted([basis[i, mode] for i in range(5)], sums if signs[mode] > 0 else gaps)
        for mode in range(10)
    ]


def x_unmodes(values, basis, signs):
    evens = [mode for mode in range(10) if signs[mode] > 0]
    odds = [mode for mode in range(10) if signs[mode] < 0]
    out = [None] * 8
    for i in range(1, 5):
        first = weighted([basis[i, mode] for mode in evens], [values[mode] for mode in evens])
        second = weighted([basis[i, mode] for mode in odds], [values[mode] for mode in odds])
        out[i - 1] = first + second
        out[8 - i] = first - second
    return out


def dot(first, second):
    return jnp.dot(first, second, preferred_element_type=F32)


def halves(values):
    high = values.astype(BF16)
    return (high, (values - high.astype(F32)).astype(BF16))


def left_mul(table, first, second):
    values = jnp.concatenate([first, second], axis=1)
    high = values.astype(BF16).astype(F32)
    rows = values.shape[0]
    parts = [high, values - high, high]
    if 3 * rows < 128:
        parts.append(jnp.zeros((128 - 3 * rows, values.shape[1]), F32))
    return dot(table, jnp.concatenate(parts, axis=0).astype(BF16))


def right_mul(values, table):
    high, low = halves(values)
    out = dot(jnp.concatenate([high, low], axis=1), table)
    return out[:, :128] + out[:, 128:]


def fold_rows(values):
    return jnp.sum(values.reshape(values.shape[0] // 8, 8, 128), axis=0)


def all_sum(values):
    lanes = jnp.sum(jnp.sum(values, axis=0, keepdims=True), axis=1, keepdims=True)
    return jnp.broadcast_to(lanes, (8, 128))


def times_tile(values, tile):
    return (values.reshape(values.shape[0] // 8, 8, 128) * tile[None]).reshape(values.shape)


def message_rows(direction, layers, extra):
    sx, sy = direction
    rows = 8 * layers if sx and sy else 32 * layers if sx else 16 * layers
    return rows + (8 if extra else 0)


def message_offsets(layers, extra):
    offsets = [0]
    for direction in DIRS:
        offsets.append(offsets[-1] + message_rows(direction, layers, extra))
    return offsets


ROUNDS = (("rhs", 2, True), ("sol", 1, False), ("sch0", 1, False), ("sti0", 2, False), ("sch1", 1, False), ("sti1", 1, False))


def body(sizes, *refs):
    n_grp, n_low, n_high = sizes
    n_dev = n_low * n_high
    (rhs_h, coef_h, sol_h, dif_h, flags_h, crow_h) = refs[:6]
    refs = refs[6:]
    tab_h = refs[: len(TABLE_NAMES)]
    refs = refs[len(TABLE_NAMES) :]
    out_p, out_r, out_s = refs[:3]
    refs = refs[3:]
    names = ("rhs", "kc", "kd", "sol", "solraw", "pin", "y1", "u", "v", "x2")
    names += ("s", "z0", "b", "p0", "w", "z1", "r1", "a1", "ct")
    buf = dict(zip(names, refs))
    refs = refs[len(names) :]
    send_bufs = dict(zip([r[0] for r in ROUNDS], refs[:6]))
    recv_bufs = dict(zip([r[0] for r in ROUNDS], refs[6:12]))
    g_send, g_recv, halo_send_sem, halo_recv_sem, g_send_sem, g_recv_sem, load_sem = refs[12:19]
    flags_ref, crow_ref = refs[19:21]
    tab = dict(zip(TABLE_NAMES, refs[21:]))

    grp = lax.axis_index("grp")
    dev = lax.axis_index("dev")
    low = lax.rem(dev, n_low)
    high = lax.div(dev, n_low)
    x_lo = jnp.where(grp > 0, 1.0, 0.0).astype(F32)
    x_hi = jnp.where(grp < n_grp - 1, 1.0, 0.0).astype(F32)
    y_lo = jnp.where(dev > 0, 1.0, 0.0).astype(F32)
    y_hi = jnp.where(dev < n_dev - 1, 1.0, 0.0).astype(F32)

    def neighbour(direction):
        return (
            lax.rem(grp + direction[0] + n_grp, n_grp),
            lax.rem(dev + direction[1] + n_dev, n_dev),
        )

    def stage_partner(stage, step):
        if stage == 0:
            return (grp, high * n_low + lax.rem(low + step, n_low))
        if stage == 1:
            return (grp, lax.rem(high + step, n_high) * n_low + low)
        return (lax.rem(grp + step, n_grp), dev)

    stage_sizes = (n_low, n_high, n_grp)

    loads = {}
    wanted = [("sol", sol_h, buf["sol"]), ("kd", dif_h, buf["kd"]), ("flags", flags_h, flags_ref)]
    wanted += [(name, source, tab[name]) for name, source in zip(TABLE_NAMES, tab_h)]
    wanted += [("rhs", rhs_h, buf["rhs"]), ("crow", crow_h, crow_ref), ("kc", coef_h, buf["kc"])]
    for at, (name, source, target) in enumerate(wanted):
        loads[name] = pltpu.make_async_copy(source, target, load_sem.at[3 + at])
        loads[name].start()

    barrier = pltpu.get_barrier_semaphore()
    greetings = 0
    for direction in DIRS:
        pl.semaphore_signal(barrier, inc=1, device_id=neighbour(direction), device_id_type=MESH_ID)
        greetings += 1
    for stage in range(3):
        for step in range(1, stage_sizes[stage]):
            pl.semaphore_signal(
                barrier, inc=1, device_id=stage_partner(stage, step), device_id_type=MESH_ID
            )
            greetings += 1

    row32 = lax.broadcasted_iota(jnp.int32, (32, 128), 0)
    lane32 = lax.broadcasted_iota(jnp.int32, (32, 128), 1)
    keep_z = jnp.where((lane32 > 0) & (lane32 < 127), 1.0, 0.0).astype(F32)
    share_z = jnp.where(((lane32 % 8 == 0) | (lane32 % 8 == 7)) & (lane32 > 0) & (lane32 < 127), 0.5, 1.0).astype(F32)
    lane_up = jnp.where((lane32 % 8 == 7) & (lane32 < 127), 1.0, 0.0).astype(F32)
    lane_down = jnp.where((lane32 % 8 == 0) & (lane32 > 0), 1.0, 0.0).astype(F32)
    row_up = jnp.where((row32 % 8 == 7) & (row32 < 31), 1.0, 0.0).astype(F32)
    row_down = jnp.where((row32 % 8 == 0) & (row32 > 0), 1.0, 0.0).astype(F32)
    edge_y = jnp.where(row32 == 0, y_lo, jnp.where(row32 == 31, y_hi, 1.0)).astype(F32)
    inner_y = jnp.where((row32 % 8 == 0) | (row32 % 8 == 7), 0.5, 1.0).astype(F32)
    face_y = jnp.where((row32 == 0) | (row32 == 31), 0.5, 1.0).astype(F32) * edge_y
    share_y = inner_y * edge_y
    tile_row = lax.broadcasted_iota(jnp.int32, (8, 128), 0)
    tile_lane = lax.broadcasted_iota(jnp.int32, (8, 128), 1)
    tile_index = tile_row * 128 + tile_lane

    def share_x(plane):
        if plane == 0:
            return 0.5 * x_lo
        if plane == 15:
            return 0.5 * x_hi
        return 0.5 if plane in (7, 8) else 1.0

    def x_times(values, factor):
        return values if isinstance(factor, float) and factor == 1.0 else values * factor

    def z_assembled(values):
        return (
            values
            + lane_up * pltpu.roll(values, 127, 1)
            + lane_down * pltpu.roll(values, 1, 1)
        )

    def y_assembled(values):
        return (
            values + row_up * pltpu.roll(values, 31, 0) + row_down * pltpu.roll(values, 1, 0)
        )

    halo_copies = {}

    def exchange(name, src, tile=None):
        at_round = [r[0] for r in ROUNDS].index(name)
        layers, extra = ROUNDS[at_round][1:]
        offsets = message_offsets(layers, extra)
        send, recv = send_bufs[name], recv_bufs[name]
        copies = []
        for at, direction in enumerate(DIRS):
            sx, sy = direction
            base = offsets[at]
            rows = message_rows(direction, layers, False)
            if sx and sy:
                for layer in range(layers):
                    plane = layer if sx < 0 else 16 - layers + layer
                    start = 32 * plane + (0 if sy < 0 else 24)
                    send[base + 8 * layer : base + 8 * layer + 8, :] = src[start : start + 8, :]
            elif sx:
                start = 0 if sx < 0 else 32 * (16 - layers)
                send[base : base + rows, :] = src[start : start + rows, :]
            else:
                for layer in range(layers):
                    row = layer if sy < 0 else 32 - layers + layer
                    send[base + 16 * layer : base + 16 * layer + 16, :] = src[
                        pl.ds(row, 16, stride=32), :
                    ]
            if extra:
                send[base + rows : base + rows + 8, :] = tile
            total = message_rows(direction, layers, extra)
            copy = pltpu.make_async_remote_copy(
                src_ref=send.at[pl.ds(base, total)],
                dst_ref=recv.at[pl.ds(base, total)],
                send_sem=halo_send_sem.at[8 * at_round + at],
                recv_sem=halo_recv_sem.at[8 * at_round + at],
                device_id=neighbour(direction),
                device_id_type=MESH_ID,
            )
            copy.start()
            copies.append(copy)
        halo_copies[name] = copies

    def arrived(name):
        for copy in halo_copies[name]:
            copy.wait_recv()

    def part(name, direction, layer=0):
        at_round = [r[0] for r in ROUNDS].index(name)
        layers, extra = ROUNDS[at_round][1:]
        offsets = message_offsets(layers, extra)
        at = DIRS.index((-direction[0], -direction[1]))
        unit = 8 if direction[0] and direction[1] else 32 if direction[0] else 16
        start = offsets[at] + unit * layer
        return recv_bufs[name][start : start + unit, :]

    def part_row(name, direction, layer, last):
        at_round = [r[0] for r in ROUNDS].index(name)
        layers, extra = ROUNDS[at_round][1:]
        at = DIRS.index((-direction[0], -direction[1]))
        start = message_offsets(layers, extra)[at] + 8 * layer + last
        return recv_bufs[name][start : start + 1, :]

    def add_faces(name, ref, masked):
        def scale(values, first, second):
            if not masked:
                return values
            return values * (first * second if first is not None and second is not None else second if first is None else first)

        ref[0:32, :] += scale(part(name, (-1, 0)), x_lo, None)
        ref[480:512, :] += scale(part(name, (1, 0)), x_hi, None)
        ref[pl.ds(0, 16, stride=32), :] += scale(part(name, (0, -1)), y_lo, None)
        ref[pl.ds(31, 16, stride=32), :] += scale(part(name, (0, 1)), y_hi, None)
        ref[0:1, :] += scale(part_row(name, (-1, -1), 0, 7), x_lo, y_lo)
        ref[31:32, :] += scale(part_row(name, (-1, 1), 0, 0), x_lo, y_hi)
        ref[480:481, :] += scale(part_row(name, (1, -1), 0, 7), x_hi, y_lo)
        ref[511:512, :] += scale(part_row(name, (1, 1), 0, 0), x_hi, y_hi)

    g_copies = []
    g_pending = {}

    def g_start(which, stage, tile):
        slot = 3 * which + stage
        g_send[8 * slot : 8 * slot + 8, :] = tile
        copies = []
        for step in range(1, stage_sizes[stage]):
            at = 7 * slot + step - 1
            copy = pltpu.make_async_remote_copy(
                src_ref=g_send.at[pl.ds(8 * slot, 8)],
                dst_ref=g_recv.at[pl.ds(8 * at, 8)],
                send_sem=g_send_sem.at[at],
                recv_sem=g_recv_sem.at[at],
                device_id=stage_partner(stage, step),
                device_id_type=MESH_ID,
            )
            copy.start()
            copies.append(copy)
        g_copies.extend(copies)
        g_pending[slot] = (tile, copies)

    def g_finish(which, stage):
        slot = 3 * which + stage
        tile, copies = g_pending[slot]
        for copy in copies:
            copy.wait_recv()
        for step in range(1, stage_sizes[stage]):
            at = 7 * slot + step - 1
            tile = tile + g_recv[8 * at : 8 * at + 8, :]
        return tile

    def g_forward(which, stage):
        g_start(which, stage + 1, g_finish(which, stage))

    def scalar_spot(at):
        return jnp.where(tile_index == 4 * 128 + at, 1.0, 0.0).astype(F32)

    def read_scalar(tile, at):
        return all_sum(tile * scalar_spot(at))

    def coarse_tile(ref):
        middle = None
        for plane in range(16):
            piece = x_times(ref[32 * plane : 32 * plane + 32, :], share_x(plane))
            middle = piece if middle is None else middle + piece
        tile = jnp.zeros((8, 128), F32)
        rows = {
            -1: ref[0:32, :] * (0.5 * x_lo),
            0: middle,
            1: ref[480:512, :] * (0.5 * x_hi),
        }
        for dx in (-1, 0, 1):
            field = rows[dx] * keep_z
            own = fold_rows(field * share_y)
            before = field[0:8] * jnp.where(tile_row == 0, 0.5 * y_lo, 0.0)
            after = field[24:32] * jnp.where(tile_row == 7, 0.5 * y_hi, 0.0)
            for dy, values in ((-1, before), (0, own), (1, after)):
                spot = lax.rem(grp + dx + n_grp, n_grp) * n_dev + lax.rem(dev + dy + n_dev, n_dev)
                tile = tile + jnp.where(tile_index == spot, all_sum(values), 0.0)
        return tile

    q_scale = 1.0 / math.sqrt(LOCAL_X * LOCAL_Y * LOCAL_Z)

    def coarse_patterns(tile):
        values = {}
        for dx in (-1, 0, 1):
            for dy in (-1, 0, 1):
                if dx == 0 and dy == 0:
                    row = buf["ct"][...]
                else:
                    direction = (dx, dy)
                    layers, extra = ROUNDS[0][1:]
                    at = DIRS.index((-dx, -dy))
                    start = message_offsets(layers, extra)[at] + message_rows((dx, dy), layers, False)
                    row = recv_bufs["rhs"][start : start + 8, :]
                values[dx, dy] = all_sum(row * tile) * q_scale
        lines = {}
        for dx in (-1, 0, 1):
            centre = jnp.concatenate([values[dx, 0]] * 4, axis=0)
            first = jnp.concatenate([values[dx, -1]] * 4, axis=0)
            last = jnp.concatenate([values[dx, 1]] * 4, axis=0)
            line = jnp.where(row32 == 0, (centre + first) * (0.5 * y_lo), centre)
            line = jnp.where(row32 == 31, (centre + last) * (0.5 * y_hi), line)
            lines[dx] = line * keep_z
        return (
            (lines[0] + lines[-1]) * (0.5 * x_lo),
            lines[0],
            (lines[0] + lines[1]) * (0.5 * x_hi),
        )

    def build_pin(name, src):
        pin = buf["pin"]
        zero8 = jnp.zeros((8, 128), F32)
        for plane in range(18):
            pin[40 * plane + 32 : 40 * plane + 40, :] = zero8
        for plane in range(16):
            pin[40 * (plane + 1) : 40 * (plane + 1) + 32, :] = src[32 * plane : 32 * plane + 32, :]
        pin[40:72, :] += part(name, (-1, 0), 1)
        pin[640:672, :] += part(name, (1, 0), 0)
        pin[pl.ds(40, 16, stride=40), :] += part(name, (0, -1), 1)
        pin[pl.ds(71, 16, stride=40), :] += part(name, (0, 1), 0)
        pin[pl.ds(72, 16, stride=40), :] = part(name, (0, -1), 0)
        pin[pl.ds(73, 16, stride=40), :] = part(name, (0, 1), 1)
        for at_plane, dx, layer in ((1, -1, 1), (16, 1, 0), (0, -1, 0), (17, 1, 1)):
            base = 40 * at_plane
            if at_plane in (0, 17):
                pin[base : base + 32, :] = part(name, (dx, 0), layer)
            pin[base : base + 1, :] += part_row(name, (dx, -1), layer, 7)
            pin[base + 31 : base + 32, :] += part_row(name, (dx, 1), layer, 0)
            pin[base + 32 : base + 33, :] += part_row(name, (dx, -1), layer, 6)
            pin[base + 33 : base + 34, :] += part_row(name, (dx, 1), layer, 1)

    row40 = lax.broadcasted_iota(jnp.int32, (40, 128), 0)
    edge40 = jnp.where(
        (row40 == 0) | (row40 == 32), y_lo, jnp.where((row40 == 31) | (row40 == 33), y_hi, 1.0)
    ).astype(F32)

    def pin_plane(plane):
        values = buf["pin"][40 * plane : 40 * plane + 40, :] * edge40
        if plane < 2:
            values = values * x_lo
        if plane > 15:
            values = values * x_hi
        return values

    def assembled_own(plane):
        return z_assembled(pin_plane(plane + 1)[0:32]) * keep_z

    basis, _ = fdm_tables()
    signs = parity_signs(basis)
    deriv = derivative_table()
    sources = ([0, 1, 2, 3, 4, 5, 6, 7, 8, 10], [7, 9, 10, 11, 12, 13, 14, 15, 16, 17])

    def schwarz(dst, hooks):
        y1, u, v, x2 = buf["y1"], buf["u"], buf["v"], buf["x2"]
        yf, yb = tab["yf"][...], tab["yb"][...]
        for pair in range(9):
            out = left_mul(yf, pin_plane(2 * pair), pin_plane(2 * pair + 1))
            y1[80 * pair : 80 * pair + 40, :] = out[0:40, :128]
            y1[80 * pair + 40 : 80 * pair + 80, :] = out[0:40, 128:]
        hooks[0]()
        for element in range(2):
            for tile in range(5):
                values = [y1[40 * p + 8 * tile : 40 * p + 8 * tile + 8, :] for p in sources[element]]
                for mode, piece in enumerate(x_modes(values, basis, signs)):
                    start = 40 * (10 * element + mode) + 8 * tile
                    u[start : start + 8, :] = piece
        for element in range(2):
            block = u[400 * element : 400 * element + 400, :]
            first, second = halves(block)
            modes = dot(jnp.concatenate([first, second], axis=1), tab["zf1"][...])
            modes = (modes + dot(first, tab["zf2"][...])) * tab["recip"][...]
            first, second = halves(modes)
            back = dot(first, tab["zb1"][...])
            v[400 * element : 400 * element + 400, :] = (
                back[:, :128] + back[:, 128:] + dot(second, tab["zb1"][:, 0:128])
            )
            hooks[1 + element]()
        for tile in range(5):
            outs = []
            for element in range(2):
                starts = [40 * (10 * element + mode) + 8 * tile for mode in range(10)]
                outs += x_unmodes([v[s : s + 8, :] for s in starts], basis, signs)
            shared = (outs[7] + outs[8]) * 0.5
            outs[7] = shared
            outs[8] = shared
            outs[0] = outs[0] * (0.5 * x_lo)
            outs[15] = outs[15] * (0.5 * x_hi)
            for plane in range(16):
                x2[40 * plane + 8 * tile : 40 * plane + 8 * tile + 8, :] = outs[plane]
        for pair in range(8):
            out = left_mul(yb, x2[80 * pair : 80 * pair + 40, :], x2[80 * pair + 40 : 80 * pair + 80, :])
            dst[64 * pair : 64 * pair + 32, :] = out[:, :128] * face_y
            dst[64 * pair + 32 : 64 * pair + 64, :] = out[:, 128:] * face_y

    def stiff(src, coef, dst, extra=None):
        energy = jnp.zeros((8, 128), F32)
        for chunk in range(2):
            at = slice(256 * chunk, 256 * chunk + 256)
            grad = right_mul(src[at, :], tab["zd"][...])
            flow = grad * coef[at, :]
            energy = energy + fold_rows(grad * flow)
            dst[at, :] = right_mul(flow, tab["zdt"][...])
        for pair in range(8):
            one = slice(64 * pair, 64 * pair + 32)
            two = slice(64 * pair + 32, 64 * pair + 64)
            grad = left_mul(tab["yd"][...], src[one, :], src[two, :])
            flow_one = grad[:, :128] * coef[one, :]
            flow_two = grad[:, 128:] * coef[two, :]
            energy = energy + fold_rows(grad[:, :128] * flow_one) + fold_rows(grad[:, 128:] * flow_two)
            back = left_mul(tab["ydt"][...], flow_one, flow_two)
            dst[one, :] += back[:, :128]
            dst[two, :] += back[:, 128:]
        for tile in range(4):
            sums = []
            for element in range(2):
                starts = [32 * (8 * element + i) + 8 * tile for i in range(8)]
                grads = x_derive([src[s : s + 8, :] for s in starts], deriv)
                flows = [grad * coef[s : s + 8, :] for grad, s in zip(grads, starts)]
                for grad, flow in zip(grads, flows):
                    energy = energy + grad * flow
                backs = x_derive(flows, deriv.T)
                for s, back in zip(starts, backs):
                    value = dst[s : s + 8, :] + back
                    if extra is not None:
                        value = value + extra[s : s + 8, :]
                    sums.append(value)
            shared = sums[7] + sums[8]
            sums[7] = shared
            sums[8] = shared
            for plane in range(16):
                dst[32 * plane + 8 * tile : 32 * plane + 8 * tile + 8, :] = sums[plane]
        for plane in range(16):
            at = slice(32 * plane, 32 * plane + 32)
            dst[at, :] = y_assembled(dst[at, :])
        return energy

    weights = GLL_WEIGHTS + GLL_WEIGHTS

    for name in ("sol", "kd", "flags", "wyz", "spread", "zd", "zdt", "yd", "ydt"):
        loads[name].wait()
    wyz = tab["wyz"][...]
    flags = jnp.concatenate([flags_ref[0], flags_ref[1]], axis=0).astype(F32).astype(BF16)
    flag_rows = dot(flags, tab["spread"][...])
    weight_column = GLL_WEIGHTS
    row8 = tile_row
    w_rows = jnp.zeros((8, 128), F32)
    for at, weight in enumerate(weight_column):
        w_rows = jnp.where(row8 == at, weight, w_rows)
    for plane in range(16):
        at = slice(32 * plane, 32 * plane + 32)
        buf["kd"][at, :] = buf["kd"][at, :] * (wyz * weights[plane])
        flux = jnp.concatenate(
            [
                flag_rows[4 * (plane // 8) + ey : 4 * (plane // 8) + ey + 1, :] * w_rows
                for ey in range(4)
            ],
            axis=0,
        )
        factor = wyz * (MASS_RATE * weights[plane]) + flux * (GROWTH * SEGREGATION * weights[plane])
        buf["x2"][at, :] = buf["sol"][at, :] * factor
    stiff(buf["sol"], buf["kd"], buf["solraw"], extra=buf["x2"])

    loads["rhs"].wait()
    loads["crow"].wait()
    for plane in range(16):
        at = slice(32 * plane, 32 * plane + 32)
        values = buf["rhs"][at, :]
        if plane == 7:
            values = values + buf["rhs"][256:288, :]
        if plane == 8:
            values = values + buf["rhs"][224:256, :]
        buf["s"][at, :] = y_assembled(values)
    ct = buf["ct"]
    ct[...] = jnp.zeros((8, 128), F32)
    count = n_grp * n_dev
    for chunk in range((count + 127) // 128):
        width = min(128, count - 128 * chunk)
        ct[chunk : chunk + 1, 0:width] = crow_ref[:, 128 * chunk : 128 * chunk + width]
    first_tile = coarse_tile(buf["s"])

    pl.semaphore_wait(barrier, greetings)
    exchange("rhs", buf["s"], ct[...])
    g_start(0, 0, first_tile)
    exchange("sol", buf["solraw"])
    for name in ("kc", "yf", "yb", "zf1", "zf2", "zb1", "recip"):
        loads[name].wait()
    for plane in range(16):
        at = slice(32 * plane, 32 * plane + 32)
        buf["kc"][at, :] = buf["kc"][at, :] * (wyz * weights[plane])

    def nothing():
        pass

    arrived("rhs")
    build_pin("rhs", buf["s"])
    g_forward(0, 0)
    schwarz(buf["z0"], (nothing, lambda: g_forward(0, 1), nothing))
    exchange("sch0", buf["z0"])
    for plane in range(16):
        buf["b"][32 * plane : 32 * plane + 32, :] = assembled_own(plane)
    total = g_finish(0, 2)
    patterns = coarse_patterns(total)

    def finish_precond(name, ref, patterns):
        arrived(name)
        add_faces(name, ref, False)
        for plane in range(16):
            at = slice(32 * plane, 32 * plane + 32)
            ref[at, :] += patterns[0 if plane == 0 else 2 if plane == 15 else 1]

    finish_precond("sch0", buf["z0"], patterns)
    share_yz = share_y * share_z

    def energy_of(first, second):
        tile = jnp.zeros((8, 128), F32)
        for plane in range(16):
            at = slice(32 * plane, 32 * plane + 32)
            piece = x_times(first[at, :] * second[at, :] * share_yz, share_x(plane))
            tile = tile + fold_rows(piece)
        return all_sum(tile)

    curve = all_sum(stiff(buf["z0"], buf["kc"], buf["a1"]))
    exchange("sti0", buf["a1"])
    rz = energy_of(buf["b"], buf["z0"])
    tile = coarse_tile(buf["a1"])
    tile = tile + scalar_spot(0) * rz + scalar_spot(1) * curve
    g_start(1, 0, tile)

    arrived("sol")
    add_faces("sol", buf["solraw"], True)
    for plane in range(16):
        at = slice(32 * plane, 32 * plane + 32)
        buf["solraw"][at, :] = z_assembled(buf["solraw"][at, :])
    store_s = pltpu.make_async_copy(buf["solraw"], out_s, load_sem.at[0])
    store_s.start()

    arrived("sti0")
    build_pin("sti0", buf["a1"])
    g_forward(1, 0)
    schwarz(buf["w"], (nothing, lambda: g_forward(1, 1), nothing))
    exchange("sch1", buf["w"])
    for plane in range(16):
        buf["p0"][32 * plane : 32 * plane + 32, :] = assembled_own(plane)
    total = g_finish(1, 2)
    patterns = coarse_patterns(total)
    rz0 = read_scalar(total, 0)
    curve0 = read_scalar(total, 1)
    alpha0 = rz0 / curve0
    for plane in range(16):
        at = slice(32 * plane, 32 * plane + 32)
        buf["r1"][at, :] = buf["b"][at, :] - times_tile(buf["p0"][at, :], alpha0)
    finish_precond("sch1", buf["w"], patterns)
    for plane in range(16):
        at = slice(32 * plane, 32 * plane + 32)
        buf["z1"][at, :] = buf["z0"][at, :] - times_tile(buf["w"][at, :], alpha0)
    curve = all_sum(stiff(buf["z1"], buf["kc"], buf["rhs"]))
    exchange("sti1", buf["rhs"])
    rz = energy_of(buf["r1"], buf["z1"])
    cross = energy_of(buf["p0"], buf["z1"])
    g_start(2, 0, scalar_spot(0) * rz + scalar_spot(1) * curve + scalar_spot(2) * cross)
    g_forward(2, 0)
    g_forward(2, 1)
    arrived("sti1")
    add_faces("sti1", buf["rhs"], False)
    for plane in range(16):
        at = slice(32 * plane, 32 * plane + 32)
        values = z_assembled(buf["rhs"][at, :]) * keep_z * edge_y
        if plane == 0:
            values = values * x_lo
        if plane == 15:
            values = values * x_hi
        buf["rhs"][at, :] = values
    total = g_finish(2, 2)
    rz1 = read_scalar(total, 0)
    curve1 = read_scalar(total, 1)
    cross1 = read_scalar(total, 2)
    beta = rz1 / rz0
    full = curve1 + 2.0 * beta * cross1 + beta * beta * curve0
    alpha1 = rz1 / full
    alpha_old = alpha0 + alpha1 * beta
    step_old = alpha1 * beta
    for plane in range(16):
        at = slice(32 * plane, 32 * plane + 32)
        buf["w"][at, :] = times_tile(buf["z0"][at, :], alpha_old) + times_tile(buf["z1"][at, :], alpha1)
        buf["r1"][at, :] = (
            buf["r1"][at, :]
            - times_tile(buf["rhs"][at, :], alpha1)
            - times_tile(buf["p0"][at, :], step_old)
        )
    store_p = pltpu.make_async_copy(buf["w"], out_p, load_sem.at[1])
    store_p.start()
    store_r = pltpu.make_async_copy(buf["r1"], out_r, load_sem.at[2])
    store_r.start()
    for name in halo_copies:
        for copy in halo_copies[name]:
            copy.wait_send()
    for copy in g_copies:
        copy.wait_send()
    store_s.wait()
    store_p.wait()
    store_r.wait()


def run_kernel(sizes, fields, flags, coarse_row, tables):
    constants = [jnp.asarray(tables[name]) for name in TABLE_NAMES]
    far = pl.BlockSpec(memory_space=pltpu.HBM)
    field = pltpu.VMEM((ROWS, LOCAL_Z), F32)

    def rows(count):
        return pltpu.VMEM((count, LOCAL_Z), F32)

    halo = [rows(message_offsets(layers, extra)[-1]) for _, layers, extra in ROUNDS]
    scratch = (
        [field] * 5
        + [rows(720), rows(720), rows(800), rows(800), rows(640)]
        + [field] * 8
        + [rows(8)]
        + halo
        + halo
        + [rows(72), rows(8 * 63)]
        + [pltpu.SemaphoreType.DMA((count,)) for count in (48, 48, 63, 63, 9 + len(constants))]
        + [pltpu.VMEM(flags.shape, jnp.int32), pltpu.VMEM(coarse_row.shape, F32)]
        + [pltpu.VMEM(table.shape, table.dtype) for table in constants]
    )
    return pl.pallas_call(
        functools.partial(body, sizes),
        out_shape=[jax.ShapeDtypeStruct((ROWS, LOCAL_Z), F32)] * 3,
        in_specs=[far] * (6 + len(constants)),
        out_specs=[far] * 3,
        scratch_shapes=scratch,
        compiler_params=pltpu.CompilerParams(
            collective_id=0, has_side_effects=True, vmem_limit_bytes=63 * 1024 * 1024
        ),
    )(*fields, flags, coarse_row, *constants)


def solution(mesh):
    n_grp, n_dev = (mesh.shape["grp"], mesh.shape["dev"])
    n_low = 8 if n_dev % 8 == 0 else 2
    sizes = (n_grp, n_low, n_dev // n_low)
    tables = make_tables()

    def shards(right_side, coefficient, solute, diffusivity, interface_flags, coarse_inverse):
        fields = [v.reshape(ROWS, LOCAL_Z) for v in (right_side, coefficient, solute, diffusivity)]
        outs = run_kernel(sizes, fields, interface_flags, coarse_inverse, tables)
        return tuple(v.reshape(LOCAL_X, LOCAL_Y, LOCAL_Z) for v in outs)

    placed = (
        P("grp", "dev", None),
        P("grp", "dev", None),
        P("grp", "dev", None),
        P("grp", "dev", None),
        P("grp", "dev", None),
        P(("grp", "dev"), None),
    )
    return jax.shard_map(
        shards,
        mesh=mesh,
        in_specs=placed,
        out_specs=(P("grp", "dev", None), P("grp", "dev", None), P("grp", "dev", None)),
        check_vma=False,
    )
```

time: 691 us -> 65 us (0.09); the launches traced: 681 us -> 64.6 us
  blocking collectives: 517 us -> 0 us
  starting transfers between devices: 97.9 us -> 0 us
  Pallas kernels: 0 us -> 60.5 us
  matrix products: 31 us -> 0 us
  local copies, waits for them, and re-layouts: 13.4 us -> 3.46 us
  between operations: 8.28 us -> 0.65 us
  other arithmetic: 7.43 us -> 0 us
    psum x3 -> x0, blocking collectives: 317 us -> none  [the longest x2 214 us: energy_sum(): lax.psum(jnp.sum(first_field * second_field * inv_mult), ('grp', 'dev'))]
    unnamed x2 -> x0, blocking collectives: 201 us -> none
    ppermute x32 -> x0, starting transfers between devices: 97.9 us -> none  [the longest x16 64.8 us: padded_2(): before = lax.ppermute(last, axis, up)]
    pallas_call x0 -> x1, Pallas kernels: none -> 60.5 us  [run_kernel(): pl.pallas_call(functools.partial(body, sizes), out_shape=[jax.ShapeDtypeS...]
    dot_general x36 -> x0, matrix products: 31 us -> none  [the longest x4 6.8 us: element_apply(): solved = jnp.einsum('pi,xaiz->xapz', table_rows, blocks, precision=HIGHEST)]
  transfers between devices with their start and end apart: 32 -> 0, of which waited for: 8 -> 0; matrix products, arithmetic and copies ran while one was open for 1% -> 0% of each run, Pallas kernels for 0% -> 0%
where the time goes in v1:
time: 65 us; the launch traced here: 64.6 us
  Pallas kernels  60.5 us (93%)
  local copies, waits for them, and re-layouts  3.46 us (5%)
  between operations  0.65 us (1%)
    pallas_call x1, Pallas kernels, run_kernel(): pl.pallas_call(functools.partial(body, sizes), out_shape=[jax.ShapeDtypeS...  60.5 us
    unnamed x7, local copies, waits for them, and re-layouts  3.46 us

profile of v1, /device:TPU:1, one launch (start us, length us, event | category | flops | bytes accessed | tf_op | source)
XLA Modules:
  0.0 64.6 jit_solution(9028526476402163709)
XLA Ops:
  0.6 60.5 %shard_map.193 = (f32[512,128]{1,0:T(8,128)}, f32[512,128]{1,0:T(8,128)}, f32[512,128]{1,0:T(8,128)}) custom-call(f32[512,128]{1,0:T(8,128)} %bitcast.7, f32[512,128]{1,0:T(8,128)} %bitcast.8, f32[512,128]{1,0:T(8,128)} %bitcast.9, f32[512,128]{1,0:T(8,128)} %bitcast.10, s32[2,4,16]{2,1,0:T(4,128)} %refs_4_.1, f32[1,512]{1,0:T(1,128)} %refs_5_.1, ...), custom_call_target="tpu_custom_call" | custom-call | tf_op jit(solution)/shard_map/pallas_call | solution.py:965
  61.2 0.0 copy-start.1
  61.2 1.7 %copy.24 = f32[16,32,128]{2,1,0:T(8,128)} copy(f32[16,32,128]{2,1,0:T(8,128)} %bitcast.13) | data formatting | bytes 524288
  62.9 0.0 copy-done.1
  62.9 0.0 copy-start
  62.9 0.7 %copy.25 = f32[16,32,128]{2,1,0:T(8,128)} copy(f32[16,32,128]{2,1,0:T(8,128)S(1)} %bitcast.12) | data formatting | bytes 524288
  63.6 0.3 copy-done
  63.9 0.7 %copy.26 = f32[16,32,128]{2,1,0:T(8,128)} copy(f32[16,32,128]{2,1,0:T(8,128)S(1)} %bitcast.11) | data formatting | bytes 524288
Async XLA Ops:
  61.2 1.7 %copy-start.1 = (f32[512,128]{1,0:T(8,128)S(1)}, f32[512,128]{1,0:T(8,128)}, u32[]{:S(2)}) copy-start(f32[512,128]{1,0:T(8,128)} %get-tuple-element.7) | copy-start | bytes 786436
  62.9 1.0 %copy-start = (f32[512,128]{1,0:T(8,128)S(1)}, f32[512,128]{1,0:T(8,128)}, u32[]{:S(2)}) copy-start(f32[512,128]{1,0:T(8,128)} %get-tuple-element.8) | copy-start | bytes 786436

commit v2 on v1

--- a/solution.py
+++ b/solution.py
@@ -169,7 +169,7 @@
 
 LOCAL_X, LOCAL_Y, LOCAL_Z = (16, 32, 128)
 ROWS = LOCAL_X * LOCAL_Y
-DIRS = ((-1, 0), (1, 0), (0, -1), (0, 1), (-1, -1), (-1, 1), (1, -1), (1, 1))
+DIRS = ((-1, -1), (-1, 1), (1, -1), (1, 1), (0, -1), (0, 1), (-1, 0), (1, 0))
 F32 = jnp.float32
 BF16 = jnp.bfloat16
 MESH_ID = pl.DeviceIdType.MESH
@@ -376,6 +376,7 @@
     return offsets
 
 
+OUT_NAMES = ("z0", "z1", "r1", "az", "p0", "sol", "steps")
 ROUNDS = (("rhs", 2, True), ("sol", 1, False), ("sch0", 1, False), ("sti0", 2, False), ("sch1", 1, False), ("sti1", 1, False))
 
 
@@ -386,61 +387,57 @@
     refs = refs[6:]
     tab_h = refs[: len(TABLE_NAMES)]
     refs = refs[len(TABLE_NAMES) :]
-    out_p, out_r, out_s = refs[:3]
-    refs = refs[3:]
+    outs = dict(zip(OUT_NAMES, refs))
+    refs = refs[len(OUT_NAMES) :]
     names = ("rhs", "kc", "kd", "sol", "solraw", "pin", "y1", "u", "v", "x2")
     names += ("s", "z0", "b", "p0", "w", "z1", "r1", "a1", "ct")
     buf = dict(zip(names, refs))
     refs = refs[len(names) :]
     send_bufs = dict(zip([r[0] for r in ROUNDS], refs[:6]))
     recv_bufs = dict(zip([r[0] for r in ROUNDS], refs[6:12]))
-    g_send, g_recv, halo_send_sem, halo_recv_sem, g_send_sem, g_recv_sem, load_sem = refs[12:19]
-    flags_ref, crow_ref = refs[19:21]
-    tab = dict(zip(TABLE_NAMES, refs[21:]))
+    g_send, g_recv, halo_send_sem, halo_recv_sem, g_send_sem, g_recv_sem = refs[12:18]
+    load_sem, store_sem, flags_ref, crow_ref, steps_ref = refs[18:23]
+    tab = dict(zip(TABLE_NAMES, refs[23:]))
 
     grp = lax.axis_index("grp")
     dev = lax.axis_index("dev")
-    low = lax.rem(dev, n_low)
-    high = lax.div(dev, n_low)
+    low = dev & (n_low - 1)
+    high = lax.shift_right_logical(dev, n_low.bit_length() - 1)
     x_lo = jnp.where(grp > 0, 1.0, 0.0).astype(F32)
     x_hi = jnp.where(grp < n_grp - 1, 1.0, 0.0).astype(F32)
     y_lo = jnp.where(dev > 0, 1.0, 0.0).astype(F32)
     y_hi = jnp.where(dev < n_dev - 1, 1.0, 0.0).astype(F32)
 
     def neighbour(direction):
-        return (
-            lax.rem(grp + direction[0] + n_grp, n_grp),
-            lax.rem(dev + direction[1] + n_dev, n_dev),
-        )
+        return ((grp + direction[0]) & (n_grp - 1), (dev + direction[1]) & (n_dev - 1))
 
     def stage_partner(stage, step):
         if stage == 0:
-            return (grp, high * n_low + lax.rem(low + step, n_low))
+            return (grp, high * n_low + ((low + step) & (n_low - 1)))
         if stage == 1:
-            return (grp, lax.rem(high + step, n_high) * n_low + low)
-        return (lax.rem(grp + step, n_grp), dev)
+            return (grp, ((high + step) & (n_high - 1)) * n_low + low)
+        return ((grp + step) & (n_grp - 1), dev)
 
     stage_sizes = (n_low, n_high, n_grp)
 
+    def steps_of(stage):
+        size = stage_sizes[stage]
+        return sorted(range(1, size), key=lambda step: -min(step, size - step))
+
+    barrier = pltpu.get_barrier_semaphore()
+    partners = [neighbour(direction) for direction in DIRS]
+    for stage in range(3):
+        partners += [stage_partner(stage, step) for step in steps_of(stage)]
+    for partner in partners:
+        pl.semaphore_signal(barrier, inc=1, device_id=partner, device_id_type=MESH_ID)
     loads = {}
-    wanted = [("sol", sol_h, buf["sol"]), ("kd", dif_h, buf["kd"]), ("flags", flags_h, flags_ref)]
+    wanted = [("rhs", rhs_h, buf["rhs"]), ("crow", crow_h, crow_ref)]
+    wanted += [("sol", sol_h, buf["sol"]), ("kd", dif_h, buf["kd"]), ("flags", flags_h, flags_ref)]
     wanted += [(name, source, tab[name]) for name, source in zip(TABLE_NAMES, tab_h)]
-    wanted += [("rhs", rhs_h, buf["rhs"]), ("crow", crow_h, crow_ref), ("kc", coef_h, buf["kc"])]
+    wanted += [("kc", coef_h, buf["kc"])]
     for at, (name, source, target) in enumerate(wanted):
-        loads[name] = pltpu.make_async_copy(source, target, load_sem.at[3 + at])
+        loads[name] = pltpu.make_async_copy(source, target, load_sem.at[at])
         loads[name].start()
-
-    barrier = pltpu.get_barrier_semaphore()
-    greetings = 0
-    for direction in DIRS:
-        pl.semaphore_signal(barrier, inc=1, device_id=neighbour(direction), device_id_type=MESH_ID)
-        greetings += 1
-    for stage in range(3):
-        for step in range(1, stage_sizes[stage]):
-            pl.semaphore_signal(
-                barrier, inc=1, device_id=stage_partner(stage, step), device_id_type=MESH_ID
-            )
-            greetings += 1
 
     row32 = lax.broadcasted_iota(jnp.int32, (32, 128), 0)
     lane32 = lax.broadcasted_iota(jnp.int32, (32, 128), 1)
@@ -556,6 +553,10 @@
         ref[480:481, :] += scale(part_row(name, (1, -1), 0, 7), x_hi, y_lo)
         ref[511:512, :] += scale(part_row(name, (1, 1), 0, 0), x_hi, y_hi)
 
+    def add_arrived(name, ref):
+        arrived(name)
+        add_faces(name, ref, False)
+
     g_copies = []
     g_pending = {}
 
@@ -563,7 +564,7 @@
         slot = 3 * which + stage
         g_send[8 * slot : 8 * slot + 8, :] = tile
         copies = []
-        for step in range(1, stage_sizes[stage]):
+        for step in steps_of(stage):
             at = 7 * slot + step - 1
             copy = pltpu.make_async_remote_copy(
                 src_ref=g_send.at[pl.ds(8 * slot, 8)],
@@ -583,7 +584,7 @@
         tile, copies = g_pending[slot]
         for copy in copies:
             copy.wait_recv()
-        for step in range(1, stage_sizes[stage]):
+        for step in steps_of(stage):
             at = 7 * slot + step - 1
             tile = tile + g_recv[8 * at : 8 * at + 8, :]
         return tile
@@ -614,7 +615,7 @@
             before = field[0:8] * jnp.where(tile_row == 0, 0.5 * y_lo, 0.0)
             after = field[24:32] * jnp.where(tile_row == 7, 0.5 * y_hi, 0.0)
             for dy, values in ((-1, before), (0, own), (1, after)):
-                spot = lax.rem(grp + dx + n_grp, n_grp) * n_dev + lax.rem(dev + dy + n_dev, n_dev)
+                spot = ((grp + dx) & (n_grp - 1)) * n_dev + ((dev + dy) & (n_dev - 1))
                 tile = tile + jnp.where(tile_index == spot, all_sum(values), 0.0)
         return tile
 
@@ -690,14 +691,13 @@
     deriv = derivative_table()
     sources = ([0, 1, 2, 3, 4, 5, 6, 7, 8, 10], [7, 9, 10, 11, 12, 13, 14, 15, 16, 17])
 
-    def schwarz(dst, hooks):
+    def schwarz(dst):
         y1, u, v, x2 = buf["y1"], buf["u"], buf["v"], buf["x2"]
         yf, yb = tab["yf"][...], tab["yb"][...]
         for pair in range(9):
             out = left_mul(yf, pin_plane(2 * pair), pin_plane(2 * pair + 1))
             y1[80 * pair : 80 * pair + 40, :] = out[0:40, :128]
             y1[80 * pair + 40 : 80 * pair + 80, :] = out[0:40, 128:]
-        hooks[0]()
         for element in range(2):
             for tile in range(5):
                 values = [y1[40 * p + 8 * tile : 40 * p + 8 * tile + 8, :] for p in sources[element]]
@@ -714,7 +714,6 @@
             v[400 * element : 400 * element + 400, :] = (
                 back[:, :128] + back[:, 128:] + dot(second, tab["zb1"][:, 0:128])
             )
-            hooks[1 + element]()
         for tile in range(5):
             outs = []
             for element in range(2):
@@ -776,6 +775,28 @@
 
     weights = GLL_WEIGHTS + GLL_WEIGHTS
 
+    loads["rhs"].wait()
+    loads["crow"].wait()
+    for plane in range(16):
+        at = slice(32 * plane, 32 * plane + 32)
+        values = buf["rhs"][at, :]
+        if plane == 7:
+            values = values + buf["rhs"][256:288, :]
+        if plane == 8:
+            values = values + buf["rhs"][224:256, :]
+        buf["s"][at, :] = y_assembled(values)
+    ct = buf["ct"]
+    ct[...] = jnp.zeros((8, 128), F32)
+    count = n_grp * n_dev
+    for chunk in range((count + 127) // 128):
+        width = min(128, count - 128 * chunk)
+        ct[chunk : chunk + 1, 0:width] = crow_ref[:, 128 * chunk : 128 * chunk + width]
+    first_tile = coarse_tile(buf["s"])
+
+    pl.semaphore_wait(barrier, len(partners))
+    g_start(0, 0, first_tile)
+    exchange("rhs", buf["s"], ct[...])
+
     for name in ("sol", "kd", "flags", "wyz", "spread", "zd", "zdt", "yd", "ydt"):
         loads[name].wait()
     wyz = tab["wyz"][...]
@@ -800,27 +821,6 @@
         buf["x2"][at, :] = buf["sol"][at, :] * factor
     stiff(buf["sol"], buf["kd"], buf["solraw"], extra=buf["x2"])
 
-    loads["rhs"].wait()
-    loads["crow"].wait()
-    for plane in range(16):
-        at = slice(32 * plane, 32 * plane + 32)
-        values = buf["rhs"][at, :]
-        if plane == 7:
-            values = values + buf["rhs"][256:288, :]
-        if plane == 8:
-            values = values + buf["rhs"][224:256, :]
-        buf["s"][at, :] = y_assembled(values)
-    ct = buf["ct"]
-    ct[...] = jnp.zeros((8, 128), F32)
-    count = n_grp * n_dev
-    for chunk in range((count + 127) // 128):
-        width = min(128, count - 128 * chunk)
-        ct[chunk : chunk + 1, 0:width] = crow_ref[:, 128 * chunk : 128 * chunk + width]
-    first_tile = coarse_tile(buf["s"])
-
-    pl.semaphore_wait(barrier, greetings)
-    exchange("rhs", buf["s"], ct[...])
-    g_start(0, 0, first_tile)
     exchange("sol", buf["solraw"])
     for name in ("kc", "yf", "yb", "zf1", "zf2", "zb1", "recip"):
         loads[name].wait()
@@ -828,27 +828,30 @@
         at = slice(32 * plane, 32 * plane + 32)
         buf["kc"][at, :] = buf["kc"][at, :] * (wyz * weights[plane])
 
-    def nothing():
-        pass
-
+    stores = []
+
+    def store(name, ref):
+        copy = pltpu.make_async_copy(ref, outs[name], store_sem.at[OUT_NAMES.index(name)])
+        copy.start()
+        stores.append(copy)
+
+    g_forward(0, 0)
     arrived("rhs")
     build_pin("rhs", buf["s"])
-    g_forward(0, 0)
-    schwarz(buf["z0"], (nothing, lambda: g_forward(0, 1), nothing))
+    schwarz(buf["z0"])
     exchange("sch0", buf["z0"])
+    g_forward(0, 1)
     for plane in range(16):
         buf["b"][32 * plane : 32 * plane + 32, :] = assembled_own(plane)
-    total = g_finish(0, 2)
-    patterns = coarse_patterns(total)
-
-    def finish_precond(name, ref, patterns):
-        arrived(name)
-        add_faces(name, ref, False)
+    add_arrived("sch0", buf["z0"])
+    patterns = coarse_patterns(g_finish(0, 2))
+
+    def finish_precond(ref, patterns):
         for plane in range(16):
             at = slice(32 * plane, 32 * plane + 32)
             ref[at, :] += patterns[0 if plane == 0 else 2 if plane == 15 else 1]
 
-    finish_precond("sch0", buf["z0"], patterns)
+    finish_precond(buf["z0"], patterns)
     share_yz = share_y * share_z
 
     def energy_of(first, second):
@@ -860,27 +863,28 @@
         return all_sum(tile)
 
     curve = all_sum(stiff(buf["z0"], buf["kc"], buf["a1"]))
-    exchange("sti0", buf["a1"])
     rz = energy_of(buf["b"], buf["z0"])
     tile = coarse_tile(buf["a1"])
     tile = tile + scalar_spot(0) * rz + scalar_spot(1) * curve
     g_start(1, 0, tile)
+    exchange("sti0", buf["a1"])
 
     arrived("sol")
     add_faces("sol", buf["solraw"], True)
     for plane in range(16):
         at = slice(32 * plane, 32 * plane + 32)
         buf["solraw"][at, :] = z_assembled(buf["solraw"][at, :])
-    store_s = pltpu.make_async_copy(buf["solraw"], out_s, load_sem.at[0])
-    store_s.start()
-
+    store("sol", buf["solraw"])
+
+    g_forward(1, 0)
     arrived("sti0")
     build_pin("sti0", buf["a1"])
-    g_forward(1, 0)
-    schwarz(buf["w"], (nothing, lambda: g_forward(1, 1), nothing))
+    schwarz(buf["w"])
     exchange("sch1", buf["w"])
+    g_forward(1, 1)
     for plane in range(16):
         buf["p0"][32 * plane : 32 * plane + 32, :] = assembled_own(plane)
+    add_arrived("sch1", buf["w"])
     total = g_finish(1, 2)
     patterns = coarse_patterns(total)
     rz0 = read_scalar(total, 0)
@@ -889,19 +893,20 @@
     for plane in range(16):
         at = slice(32 * plane, 32 * plane + 32)
         buf["r1"][at, :] = buf["b"][at, :] - times_tile(buf["p0"][at, :], alpha0)
-    finish_precond("sch1", buf["w"], patterns)
+    finish_precond(buf["w"], patterns)
     for plane in range(16):
         at = slice(32 * plane, 32 * plane + 32)
         buf["z1"][at, :] = buf["z0"][at, :] - times_tile(buf["w"][at, :], alpha0)
     curve = all_sum(stiff(buf["z1"], buf["kc"], buf["rhs"]))
-    exchange("sti1", buf["rhs"])
     rz = energy_of(buf["r1"], buf["z1"])
     cross = energy_of(buf["p0"], buf["z1"])
     g_start(2, 0, scalar_spot(0) * rz + scalar_spot(1) * curve + scalar_spot(2) * cross)
+    exchange("sti1", buf["rhs"])
+    for name in ("z0", "z1", "r1", "p0"):
+        store(name, buf[name])
     g_forward(2, 0)
+    add_arrived("sti1", buf["rhs"])
     g_forward(2, 1)
-    arrived("sti1")
-    add_faces("sti1", buf["rhs"], False)
     for plane in range(16):
         at = slice(32 * plane, 32 * plane + 32)
         values = z_assembled(buf["rhs"][at, :]) * keep_z * edge_y
@@ -910,6 +915,7 @@
         if plane == 15:
             values = values * x_hi
         buf["rhs"][at, :] = values
+    store("az", buf["rhs"])
     total = g_finish(2, 2)
     rz1 = read_scalar(total, 0)
     curve1 = read_scalar(total, 1)
@@ -917,28 +923,60 @@
     beta = rz1 / rz0
     full = curve1 + 2.0 * beta * cross1 + beta * beta * curve0
     alpha1 = rz1 / full
-    alpha_old = alpha0 + alpha1 * beta
-    step_old = alpha1 * beta
-    for plane in range(16):
-        at = slice(32 * plane, 32 * plane + 32)
-        buf["w"][at, :] = times_tile(buf["z0"][at, :], alpha_old) + times_tile(buf["z1"][at, :], alpha1)
-        buf["r1"][at, :] = (
-            buf["r1"][at, :]
-            - times_tile(buf["rhs"][at, :], alpha1)
-            - times_tile(buf["p0"][at, :], step_old)
-        )
-    store_p = pltpu.make_async_copy(buf["w"], out_p, load_sem.at[1])
-    store_p.start()
-    store_r = pltpu.make_async_copy(buf["r1"], out_r, load_sem.at[2])
-    store_r.start()
+    steps_ref[0:8, :] = alpha0 + alpha1 * beta
+    steps_ref[8:16, :] = alpha1
+    steps_ref[16:24, :] = alpha1 * beta
+    store("steps", steps_ref)
     for name in halo_copies:
         for copy in halo_copies[name]:
             copy.wait_send()
     for copy in g_copies:
         copy.wait_send()
-    store_s.wait()
-    store_p.wait()
-    store_r.wait()
+    for copy in stores:
+        copy.wait()
+
+
+def finish_body(*refs):
+    count = len(OUT_NAMES)
+    sources, targets, bufs, load_sem, store_sem = refs[:count], refs[count : count + 3], refs[count + 3 : 2 * count + 3], refs[-2], refs[-1]
+    loads = {}
+    for at in (6, 0, 1, 2, 3, 4, 5):
+        loads[OUT_NAMES[at]] = pltpu.make_async_copy(sources[at], bufs[at], load_sem.at[at])
+        loads[OUT_NAMES[at]].start()
+    z0, z1, r1, az, p0, sol, steps = bufs
+    for name in ("steps", "z0", "z1"):
+        loads[name].wait()
+    old, new, back = steps[0:8, :], steps[8:16, :], steps[16:24, :]
+    for plane in range(LOCAL_X):
+        at = slice(32 * plane, 32 * plane + 32)
+        z0[at, :] = times_tile(z0[at, :], old) + times_tile(z1[at, :], new)
+    stores = [pltpu.make_async_copy(z0, targets[0], store_sem.at[0])]
+    stores[0].start()
+    for name in ("r1", "az", "p0"):
+        loads[name].wait()
+    for plane in range(LOCAL_X):
+        at = slice(32 * plane, 32 * plane + 32)
+        r1[at, :] = r1[at, :] - times_tile(az[at, :], new) - times_tile(p0[at, :], back)
+    stores.append(pltpu.make_async_copy(r1, targets[1], store_sem.at[1]))
+    stores[1].start()
+    loads["sol"].wait()
+    stores.append(pltpu.make_async_copy(sol, targets[2], store_sem.at[2]))
+    stores[2].start()
+    for copy in stores:
+        copy.wait()
+
+
+def finish(fields):
+    far = pl.BlockSpec(memory_space=pltpu.HBM)
+    return pl.pallas_call(
+        finish_body,
+        out_shape=[jax.ShapeDtypeStruct((ROWS, LOCAL_Z), F32)] * 3,
+        in_specs=[far] * len(OUT_NAMES),
+        out_specs=[far] * 3,
+        scratch_shapes=[pltpu.VMEM(v.shape, F32) for v in fields]
+        + [pltpu.SemaphoreType.DMA((len(OUT_NAMES),)), pltpu.SemaphoreType.DMA((3,))],
+        compiler_params=pltpu.CompilerParams(vmem_limit_bytes=63 * 1024 * 1024),
+    )(*fields)
 
 
 def run_kernel(sizes, fields, flags, coarse_row, tables):
@@ -958,15 +996,17 @@
         + halo
         + halo
         + [rows(72), rows(8 * 63)]
-        + [pltpu.SemaphoreType.DMA((count,)) for count in (48, 48, 63, 63, 9 + len(constants))]
-        + [pltpu.VMEM(flags.shape, jnp.int32), pltpu.VMEM(coarse_row.shape, F32)]
+        + [pltpu.SemaphoreType.DMA((count,)) for count in (48, 48, 63, 63, 6 + len(constants), len(OUT_NAMES))]
+        + [pltpu.VMEM(flags.shape, jnp.int32), pltpu.VMEM(coarse_row.shape, F32), rows(24)]
         + [pltpu.VMEM(table.shape, table.dtype) for table in constants]
     )
     return pl.pallas_call(
         functools.partial(body, sizes),
-        out_shape=[jax.ShapeDtypeStruct((ROWS, LOCAL_Z), F32)] * 3,
+        out_shape=[
+            jax.ShapeDtypeStruct((24 if name == "steps" else ROWS, LOCAL_Z), F32) for name in OUT_NAMES
+        ],
         in_specs=[far] * (6 + len(constants)),
-        out_specs=[far] * 3,
+        out_specs=[far] * len(OUT_NAMES),
         scratch_shapes=scratch,
         compiler_params=pltpu.CompilerParams(
             collective_id=0, has_side_effects=True, vmem_limit_bytes=63 * 1024 * 1024
@@ -983,7 +1023,7 @@
     def shards(right_side, coefficient, solute, diffusivity, interface_flags, coarse_inverse):
         fields = [v.reshape(ROWS, LOCAL_Z) for v in (right_side, coefficient, solute, diffusivity)]
         outs = run_kernel(sizes, fields, interface_flags, coarse_inverse, tables)
-        return tuple(v.reshape(LOCAL_X, LOCAL_Y, LOCAL_Z) for v in outs)
+        return tuple(v.reshape(LOCAL_X, LOCAL_Y, LOCAL_Z) for v in finish(outs))
 
     placed = (
         P("grp", "dev", None),

time: 65 us -> 58.9 us (0.906)
  local copies, waits for them, and re-layouts: 3.46 us -> 0 us
  Pallas kernels: 60.5 us -> 58 us
    pallas_call x1, Pallas kernels: 60.5 us -> 55.8 us  [run_kernel(): pl.pallas_call(functools.partial(body, sizes), out_shape=[jax.ShapeDtypeS...]
    unnamed x7 -> x0, local copies, waits for them, and re-layouts: 3.46 us -> none
    pallas_call x0 -> x1, Pallas kernels: none -> 2.2 us  [finish(): pl.pallas_call(finish_body, out_shape=[jax.ShapeDtypeStruct((ROWS, LOCAL_...]
where the time goes in v2:
time: 58.9 us; the launch traced here: 58.7 us
  Pallas kernels  58 us (98%)
  between operations  0.64 us (1%)
    pallas_call x1, Pallas kernels, run_kernel(): pl.pallas_call(functools.partial(body, sizes), out_shape=[jax.ShapeDtypeS...  55.8 us
    pallas_call x1, Pallas kernels, finish(): pl.pallas_call(finish_body, out_shape=[jax.ShapeDtypeStruct((ROWS, LOCAL_...  2.2 us

profile of v2, /device:TPU:1, one launch (start us, length us, event | category | flops | bytes accessed | tf_op | source)
XLA Modules:
  0.0 58.7 jit_solution(11185877341858469689)
XLA Ops:
  0.6 55.8 %shard_map.193 = (f32[512,128]{1,0:T(8,128)}, f32[512,128]{1,0:T(8,128)}, f32[512,128]{1,0:T(8,128)}, f32[512,128]{1,0:T(8,128)}, f32[512,128]{1,0:T(8,128)}, /*index=5*/f32[512,128]{1,0:T(8,128)}, f32[24,128]{1,0:T(8,128)}) custom-call(f32[512,128]{1,0:T(8,128)} %bitcast.7, f32[512,128]{1,0:T(8,128)} %bitcast.8, f32[512,128]{1,0:T(8,128)} %bitcast.9, ...), custom_call_target="tpu_custom_call" | custom-call | tf_op jit(solution)/shard_map/pallas_call | solution.py:1003
  56.5 2.2 %shard_map.194 = (f32[512,128]{1,0:T(8,128)}, f32[512,128]{1,0:T(8,128)}, f32[512,128]{1,0:T(8,128)}) custom-call(f32[512,128]{1,0:T(8,128)} %get-tuple-element.13.refs_0_, f32[512,128]{1,0:T(8,128)} %get-tuple-element.14.refs_1_, f32[512,128]{1,0:T(8,128)} %get-tuple-element.15.refs_2_, f32[512,128]{1,0:T(8,128)} %get-tuple-element.16.refs_3_, ...), custom_call_target="tpu_custom_call" | custom-call | tf_op jit(solution)/shard_map/pallas_call | solution.py:971

commit v3 on v2

--- a/solution.py
+++ b/solution.py
@@ -253,6 +253,11 @@
     recip[:, :160] = (1.0 / sums).reshape(400, 160)
     weights = np.array(GLL_WEIGHTS)
     wyz = np.tile(weights, count_y)[:, None] * np.tile(weights, LOCAL_Z // 8)[None, :]
+    steep = np.zeros((24, LOCAL_Z), np.float32)
+    steep[0:8, 0:8] = deriv[:, 0] ** 2
+    steep[0:8, LOCAL_Z - 8 :] = deriv[:, 7] ** 2
+    steep[8:16] = deriv[:, 0:1] ** 2
+    steep[16:24] = deriv[:, 7:8] ** 2
     spread = np.zeros((LOCAL_Z // 8, LOCAL_Z), ml_dtypes.bfloat16)
     for element in range(LOCAL_Z // 8):
         spread[element, 8 * element] = 1.0
@@ -268,11 +273,12 @@
         zdt=square(deriv_z.T),
         wyz=wyz.astype(np.float32),
         spread=spread,
+        steep=steep,
         recip=recip,
     )
 
 
-TABLE_NAMES = ("yf", "yb", "yd", "ydt", "zf1", "zf2", "zb1", "zd", "zdt", "wyz", "spread", "recip")
+TABLE_NAMES = ("yf", "yb", "yd", "ydt", "zf1", "zf2", "zb1", "zd", "zdt", "wyz", "spread", "steep", "recip")
 
 
 def parity_signs(basis):
@@ -376,7 +382,7 @@
     return offsets
 
 
-OUT_NAMES = ("z0", "z1", "r1", "az", "p0", "sol", "steps")
+OUT_NAMES = ("z0", "w", "b", "aw", "p0", "sol", "steps")
 ROUNDS = (("rhs", 2, True), ("sol", 1, False), ("sch0", 1, False), ("sti0", 2, False), ("sch1", 1, False), ("sti1", 1, False))
 
 
@@ -390,7 +396,7 @@
     outs = dict(zip(OUT_NAMES, refs))
     refs = refs[len(OUT_NAMES) :]
     names = ("rhs", "kc", "kd", "sol", "solraw", "pin", "y1", "u", "v", "x2")
-    names += ("s", "z0", "b", "p0", "w", "z1", "r1", "a1", "ct")
+    names += ("s", "z0", "b", "p0", "w", "a1", "ct")
     buf = dict(zip(names, refs))
     refs = refs[len(names) :]
     send_bufs = dict(zip([r[0] for r in ROUNDS], refs[:6]))
@@ -559,81 +565,231 @@
 
     g_copies = []
     g_pending = {}
-
-    def g_start(which, stage, tile):
+    reach = n_low + 2
+
+    def g_send_rows(which, stage, values):
         slot = 3 * which + stage
-        g_send[8 * slot : 8 * slot + 8, :] = tile
-        copies = []
+        rows = values.shape[0]
+        g_send[8 * slot : 8 * slot + rows, :] = values
+        copies = {}
         for step in steps_of(stage):
             at = 7 * slot + step - 1
             copy = pltpu.make_async_remote_copy(
-                src_ref=g_send.at[pl.ds(8 * slot, 8)],
-                dst_ref=g_recv.at[pl.ds(8 * at, 8)],
+                src_ref=g_send.at[pl.ds(8 * slot, rows)],
+                dst_ref=g_recv.at[pl.ds(8 * at, rows)],
                 send_sem=g_send_sem.at[at],
                 recv_sem=g_recv_sem.at[at],
                 device_id=stage_partner(stage, step),
                 device_id_type=MESH_ID,
             )
             copy.start()
-            copies.append(copy)
-        g_copies.extend(copies)
-        g_pending[slot] = (tile, copies)
-
-    def g_finish(which, stage):
+            copies[step] = copy
+        g_copies.extend(copies.values())
+        g_pending[slot] = (values, copies)
+
+    def g_rows(which, stage):
         slot = 3 * which + stage
-        tile, copies = g_pending[slot]
-        for copy in copies:
-            copy.wait_recv()
+        values, copies = g_pending[slot]
+        out = {0: values}
+        for step in reversed(steps_of(stage)):
+            copies[step].wait_recv()
         for step in steps_of(stage):
             at = 7 * slot + step - 1
-            tile = tile + g_recv[8 * at : 8 * at + 8, :]
-        return tile
-
-    def g_forward(which, stage):
-        g_start(which, stage + 1, g_finish(which, stage))
-
-    def scalar_spot(at):
-        return jnp.where(tile_index == 4 * 128 + at, 1.0, 0.0).astype(F32)
+            out[step] = g_recv[8 * at : 8 * at + values.shape[0], :]
+        return out
+
+    def total_of(rows):
+        total = None
+        for values in rows.values():
+            total = values if total is None else total + values
+        return total
+
+    def scalar_spot(start, at):
+        return tile_lane == start + at
+
+    def g_start(which, sums, scalars):
+        tile = jnp.zeros((8, 128), F32)
+        for (dx, dy), value in sums.items():
+            tile = jnp.where(tile_lane == reach * (dx + 1) + low + dy + 1, value, tile)
+        for at, value in enumerate(scalars):
+            tile = jnp.where(scalar_spot(32, at), value, tile)
+        g_send_rows(which, 0, tile[0:1])
+
+    lane2 = lax.broadcasted_iota(jnp.int32, (1, 128), 1)
+
+    def g_second(which):
+        row = total_of(g_rows(which, 0))
+
+        def moved(part, base):
+            inside = (lane2 >= reach * part) & (lane2 < reach * (part + 1))
+            shift = (high * n_low + (base - 1 - reach * part) + 256) & 127
+            return pltpu.roll(jnp.where(inside, row, 0.0), shift, 1)
+
+        scalars = pltpu.roll(jnp.where(lane2 >= 32, row, 0.0), 32, 1)
+        scalars = jnp.where((lane2 >= 64) & (lane2 < 72), scalars, 0.0)
+        one = moved(0, 0) + moved(1, 64)
+        two = moved(2, 0) + scalars
+        g_send_rows(which, 1, jnp.concatenate([one, two], axis=0))
+
+    def g_third(which):
+        g_send_rows(which, 2, total_of(g_rows(which, 1)))
+
+    def g_finish(which):
+        rows = g_rows(which, 2)
+        sides = jnp.zeros((8, 128), F32)
+        middle = jnp.zeros((8, 128), F32)
+        scalars = None
+        for step, values in rows.items():
+            source = (grp - step) & (n_grp - 1)
+            one = jnp.broadcast_to(values[0:1], (8, 128))
+            two = jnp.broadcast_to(values[1:2], (8, 128))
+            sides = sides + jnp.where(tile_row == ((source - 1) & (n_grp - 1)), one, 0.0)
+            sides = sides + jnp.where(tile_row == ((source + 1) & (n_grp - 1)), two, 0.0)
+            middle = middle + jnp.where(tile_row == source, one, 0.0)
+            scalars = two if scalars is None else scalars + two
+        return (sides + pltpu.roll(middle, 64, 1), scalars)
 
     def read_scalar(tile, at):
-        return all_sum(tile * scalar_spot(at))
-
-    def coarse_tile(ref):
+        lanes = jnp.sum(jnp.where(tile_lane == at, tile, 0.0), axis=1, keepdims=True)
+        return jnp.broadcast_to(lanes, (8, 128))
+
+    def coarse_sums(ref):
         middle = None
         for plane in range(16):
             piece = x_times(ref[32 * plane : 32 * plane + 32, :], share_x(plane))
             middle = piece if middle is None else middle + piece
-        tile = jnp.zeros((8, 128), F32)
         rows = {
             -1: ref[0:32, :] * (0.5 * x_lo),
             0: middle,
             1: ref[480:512, :] * (0.5 * x_hi),
         }
+        sums = {}
         for dx in (-1, 0, 1):
             field = rows[dx] * keep_z
-            own = fold_rows(field * share_y)
-            before = field[0:8] * jnp.where(tile_row == 0, 0.5 * y_lo, 0.0)
-            after = field[24:32] * jnp.where(tile_row == 7, 0.5 * y_hi, 0.0)
-            for dy, values in ((-1, before), (0, own), (1, after)):
-                spot = ((grp + dx) & (n_grp - 1)) * n_dev + ((dev + dy) & (n_dev - 1))
-                tile = tile + jnp.where(tile_index == spot, all_sum(values), 0.0)
-        return tile
+            sums[dx, 0] = all_sum(fold_rows(field * share_y))
+            sums[dx, -1] = all_sum(field[0:8] * jnp.where(tile_row == 0, 0.5 * y_lo, 0.0))
+            sums[dx, 1] = all_sum(field[24:32] * jnp.where(tile_row == 7, 0.5 * y_hi, 0.0))
+        return sums
+
+    def mass_kind(one, two):
+        if one == "c":
+            return two
+        return one if two in ("c", one) else None
+
+    def steep_kind(one, two):
+        return "d" + one if one == two != "c" else None
+
+    def coarse_energies():
+        coef = buf["kc"]
+        steep_z, steep_first, steep_last = [tab["steep"][8 * i : 8 * i + 8, :] for i in range(3)]
+        planes = [coef[32 * plane : 32 * plane + 32, :] for plane in range(16)]
+        along_x = {
+            "c": weighted([1.0] * 16, planes),
+            "0": planes[0],
+            "1": planes[15],
+            "d0": weighted(deriv[:, 0] ** 2, planes[:8]),
+            "d1": weighted(deriv[:, 7] ** 2, planes[8:]),
+        }
+        z_mass = keep_z[0:8]
+
+        def reduced(x_kind, y_kind, z_part):
+            values = along_x[x_kind]
+            if y_kind == "c":
+                values = fold_rows(values)
+            elif y_kind == "0":
+                values = jnp.where(tile_row == 0, values[0:8], 0.0)
+            elif y_kind == "1":
+                values = jnp.where(tile_row == 7, values[24:32], 0.0)
+            elif y_kind == "d0":
+                values = values[0:8] * steep_first
+            else:
+                values = values[24:32] * steep_last
+            return all_sum(values * z_part)
+
+        kinds = ("c", "0", "1")
+        pieces = {}
+        for one in kinds:
+            for two in kinds:
+                pieces[one, two] = reduced(one, two, steep_z)
+        for steep in ("d0", "d1"):
+            for kind in kinds:
+                pieces[steep, kind] = reduced(steep, kind, z_mass)
+                pieces[kind, steep] = reduced(kind, steep, z_mass)
+        energies = {}
+        for a in kinds:
+            for b in kinds:
+                for c in kinds:
+                    for d in kinds:
+                        keys = (
+                            (mass_kind(a, c), mass_kind(b, d)),
+                            (steep_kind(a, c), mass_kind(b, d)),
+                            (mass_kind(a, c), steep_kind(b, d)),
+                        )
+                        found = [pieces[key] for key in keys if key in pieces]
+                        if found:
+                            energies[a, b, c, d] = weighted([1.0] * len(found), found)
+        return energies
+
+    def coarse_image(energies, values):
+        kinds = ("c", "0", "1")
+        half_x = (0.5 * x_lo, 0.5 * x_hi)
+        half_y = (0.5 * y_lo, 0.5 * y_hi)
+
+        def split(before, own, after, half):
+            return {
+                "c": own,
+                "0": before * half[0] + own * (half[0] - 1.0),
+                "1": after * half[1] + own * (half[1] - 1.0),
+            }
+
+        def joined(parts, half):
+            own = parts["c"] + parts["0"] * (half[0] - 1.0) + parts["1"] * (half[1] - 1.0)
+            return (parts["0"] * half[0], own, parts["1"] * half[1])
+
+        by_x = {dy: split(*[values[dx, dy] for dx in (-1, 0, 1)], half_x) for dy in (-1, 0, 1)}
+        steps = {a: split(*[by_x[dy][a] for dy in (-1, 0, 1)], half_y) for a in kinds}
+        image = {}
+        for a in kinds:
+            parts = {}
+            for b in kinds:
+                terms = [
+                    energies[a, b, c, d] * steps[c][d]
+                    for c in kinds
+                    for d in kinds
+                    if (a, b, c, d) in energies
+                ]
+                parts[b] = weighted([1.0] * len(terms), terms)
+            image[a] = joined(parts, half_y)
+        out = {}
+        for at, dy in enumerate((-1, 0, 1)):
+            for dx, value in zip((-1, 0, 1), joined({a: image[a][at] for a in kinds}, half_x)):
+                out[dx, dy] = value
+        return out
+
+    def paired(values, sums):
+        total = None
+        for key in values:
+            piece = values[key] * sums[key]
+            total = piece if total is None else total + piece
+        return total
 
     q_scale = 1.0 / math.sqrt(LOCAL_X * LOCAL_Y * LOCAL_Z)
 
-    def coarse_patterns(tile):
+    def coarse_values(tile):
         values = {}
         for dx in (-1, 0, 1):
             for dy in (-1, 0, 1):
                 if dx == 0 and dy == 0:
                     row = buf["ct"][...]
                 else:
-                    direction = (dx, dy)
                     layers, extra = ROUNDS[0][1:]
                     at = DIRS.index((-dx, -dy))
                     start = message_offsets(layers, extra)[at] + message_rows((dx, dy), layers, False)
                     row = recv_bufs["rhs"][start : start + 8, :]
                 values[dx, dy] = all_sum(row * tile) * q_scale
+        return values
+
+    def coarse_patterns(values):
         lines = {}
         for dx in (-1, 0, 1):
             centre = jnp.concatenate([values[dx, 0]] * 4, axis=0)
@@ -788,13 +944,19 @@
     ct = buf["ct"]
     ct[...] = jnp.zeros((8, 128), F32)
     count = n_grp * n_dev
-    for chunk in range((count + 127) // 128):
-        width = min(128, count - 128 * chunk)
-        ct[chunk : chunk + 1, 0:width] = crow_ref[:, 128 * chunk : 128 * chunk + width]
-    first_tile = coarse_tile(buf["s"])
+    for at in range(n_grp):
+        start = n_dev * at
+        if count >= 128:
+            row = crow_ref[:, start // 128 * 128 : start // 128 * 128 + 128]
+        else:
+            row = jnp.concatenate([crow_ref[...], jnp.zeros((1, 128 - count), F32)], axis=1)
+        if start % 128:
+            row = pltpu.roll(row, 128 - start % 128, 1)
+        ct[at : at + 1, :] = jnp.where(lane2 < n_dev, row, 0.0)
+    right_sums = coarse_sums(buf["s"])
 
     pl.semaphore_wait(barrier, len(partners))
-    g_start(0, 0, first_tile)
+    g_start(0, right_sums, [])
     exchange("rhs", buf["s"], ct[...])
 
     for name in ("sol", "kd", "flags", "wyz", "spread", "zd", "zdt", "yd", "ydt"):
@@ -822,11 +984,12 @@
     stiff(buf["sol"], buf["kd"], buf["solraw"], extra=buf["x2"])
 
     exchange("sol", buf["solraw"])
-    for name in ("kc", "yf", "yb", "zf1", "zf2", "zb1", "recip"):
+    for name in ("kc", "steep", "yf", "yb", "zf1", "zf2", "zb1", "recip"):
         loads[name].wait()
     for plane in range(16):
         at = slice(32 * plane, 32 * plane + 32)
         buf["kc"][at, :] = buf["kc"][at, :] * (wyz * weights[plane])
+    energies = coarse_energies()
 
     stores = []
 
@@ -835,26 +998,17 @@
         copy.start()
         stores.append(copy)
 
-    g_forward(0, 0)
+    g_second(0)
     arrived("rhs")
     build_pin("rhs", buf["s"])
     schwarz(buf["z0"])
     exchange("sch0", buf["z0"])
-    g_forward(0, 1)
+    g_third(0)
     for plane in range(16):
         buf["b"][32 * plane : 32 * plane + 32, :] = assembled_own(plane)
-    add_arrived("sch0", buf["z0"])
-    patterns = coarse_patterns(g_finish(0, 2))
-
-    def finish_precond(ref, patterns):
-        for plane in range(16):
-            at = slice(32 * plane, 32 * plane + 32)
-            ref[at, :] += patterns[0 if plane == 0 else 2 if plane == 15 else 1]
-
-    finish_precond(buf["z0"], patterns)
     share_yz = share_y * share_z
 
-    def energy_of(first, second):
+    def product_of(first, second):
         tile = jnp.zeros((8, 128), F32)
         for plane in range(16):
             at = slice(32 * plane, 32 * plane + 32)
@@ -862,11 +1016,25 @@
             tile = tile + fold_rows(piece)
         return all_sum(tile)
 
+    def add_coarse(ref, values):
+        patterns = coarse_patterns(values)
+        for plane in range(16):
+            at = slice(32 * plane, 32 * plane + 32)
+            ref[at, :] += patterns[0 if plane == 0 else 2 if plane == 15 else 1]
+
+    add_arrived("sch0", buf["z0"])
     curve = all_sum(stiff(buf["z0"], buf["kc"], buf["a1"]))
-    rz = energy_of(buf["b"], buf["z0"])
-    tile = coarse_tile(buf["a1"])
-    tile = tile + scalar_spot(0) * rz + scalar_spot(1) * curve
-    g_start(1, 0, tile)
+    sums = coarse_sums(buf["a1"])
+    rz = product_of(buf["b"], buf["z0"])
+    total, _ = g_finish(0)
+    coarse = coarse_values(total)
+    image = coarse_image(energies, coarse)
+    applied_sums = {key: sums[key] + image[key] for key in sums}
+    rz = rz + paired(coarse, right_sums)
+    curve = curve + paired(coarse, {key: sums[key] + applied_sums[key] for key in sums})
+    g_start(1, applied_sums, [rz, curve])
+    add_coarse(buf["z0"], coarse)
+    stiff(buf["z0"], buf["kc"], buf["a1"])
     exchange("sti0", buf["a1"])
 
     arrived("sol")
@@ -876,37 +1044,40 @@
         buf["solraw"][at, :] = z_assembled(buf["solraw"][at, :])
     store("sol", buf["solraw"])
 
-    g_forward(1, 0)
+    g_second(1)
     arrived("sti0")
     build_pin("sti0", buf["a1"])
     schwarz(buf["w"])
     exchange("sch1", buf["w"])
-    g_forward(1, 1)
+    g_third(1)
     for plane in range(16):
         buf["p0"][32 * plane : 32 * plane + 32, :] = assembled_own(plane)
     add_arrived("sch1", buf["w"])
-    total = g_finish(1, 2)
-    patterns = coarse_patterns(total)
-    rz0 = read_scalar(total, 0)
-    curve0 = read_scalar(total, 1)
+    w_curve = all_sum(stiff(buf["w"], buf["kc"], buf["rhs"]))
+    sums = coarse_sums(buf["rhs"])
+    b_w = product_of(buf["b"], buf["w"])
+    p_w = product_of(buf["p0"], buf["w"])
+    total, scalars = g_finish(1)
+    coarse = coarse_values(total)
+    image = coarse_image(energies, coarse)
+    b_w = b_w + paired(coarse, right_sums)
+    p_w = p_w + paired(coarse, applied_sums)
+    w_curve = w_curve + paired(coarse, {key: 2.0 * sums[key] + image[key] for key in sums})
+    tile = jnp.zeros((8, 128), F32)
+    for at, value in enumerate((b_w, p_w, w_curve)):
+        tile = jnp.where(tile_lane == at, value, tile)
+    g_send_rows(2, 0, tile[0:1])
+    rz0 = read_scalar(scalars, 64)
+    curve0 = read_scalar(scalars, 65)
     alpha0 = rz0 / curve0
-    for plane in range(16):
-        at = slice(32 * plane, 32 * plane + 32)
-        buf["r1"][at, :] = buf["b"][at, :] - times_tile(buf["p0"][at, :], alpha0)
-    finish_precond(buf["w"], patterns)
-    for plane in range(16):
-        at = slice(32 * plane, 32 * plane + 32)
-        buf["z1"][at, :] = buf["z0"][at, :] - times_tile(buf["w"][at, :], alpha0)
-    curve = all_sum(stiff(buf["z1"], buf["kc"], buf["rhs"]))
-    rz = energy_of(buf["r1"], buf["z1"])
-    cross = energy_of(buf["p0"], buf["z1"])
-    g_start(2, 0, scalar_spot(0) * rz + scalar_spot(1) * curve + scalar_spot(2) * cross)
+    add_coarse(buf["w"], coarse)
+    stiff(buf["w"], buf["kc"], buf["rhs"])
     exchange("sti1", buf["rhs"])
-    for name in ("z0", "z1", "r1", "p0"):
+    for name in ("z0", "w", "b", "p0"):
         store(name, buf[name])
-    g_forward(2, 0)
+    g_send_rows(2, 1, total_of(g_rows(2, 0)))
     add_arrived("sti1", buf["rhs"])
-    g_forward(2, 1)
+    g_send_rows(2, 2, total_of(g_rows(2, 1)))
     for plane in range(16):
         at = slice(32 * plane, 32 * plane + 32)
         values = z_assembled(buf["rhs"][at, :]) * keep_z * edge_y
@@ -915,17 +1086,16 @@
         if plane == 15:
             values = values * x_hi
         buf["rhs"][at, :] = values
-    store("az", buf["rhs"])
-    total = g_finish(2, 2)
-    rz1 = read_scalar(total, 0)
-    curve1 = read_scalar(total, 1)
-    cross1 = read_scalar(total, 2)
+    store("aw", buf["rhs"])
+    total = jnp.broadcast_to(total_of(g_rows(2, 2)), (8, 128))
+    b_w, p_w, w_curve = [read_scalar(total, at) for at in range(3)]
+    rz1 = alpha0 * (alpha0 * p_w - b_w)
+    cross1 = curve0 - alpha0 * p_w
+    curve1 = cross1 - alpha0 * (p_w - alpha0 * w_curve)
     beta = rz1 / rz0
-    full = curve1 + 2.0 * beta * cross1 + beta * beta * curve0
-    alpha1 = rz1 / full
-    steps_ref[0:8, :] = alpha0 + alpha1 * beta
-    steps_ref[8:16, :] = alpha1
-    steps_ref[16:24, :] = alpha1 * beta
+    alpha1 = rz1 / (curve1 + beta * (2.0 * cross1 + beta * curve0))
+    steps_ref[0:8, :] = alpha0 + alpha1 * (1.0 + beta)
+    steps_ref[8:16, :] = alpha0 * alpha1
     store("steps", steps_ref)
     for name in halo_copies:
         for copy in halo_copies[name]:
@@ -943,21 +1113,21 @@
     for at in (6, 0, 1, 2, 3, 4, 5):
         loads[OUT_NAMES[at]] = pltpu.make_async_copy(sources[at], bufs[at], load_sem.at[at])
         loads[OUT_NAMES[at]].start()
-    z0, z1, r1, az, p0, sol, steps = bufs
-    for name in ("steps", "z0", "z1"):
+    z0, w, b, aw, p0, sol, steps = bufs
+    for name in ("steps", "z0", "w"):
         loads[name].wait()
-    old, new, back = steps[0:8, :], steps[8:16, :], steps[16:24, :]
+    first, second = steps[0:8, :], steps[8:16, :]
     for plane in range(LOCAL_X):
         at = slice(32 * plane, 32 * plane + 32)
-        z0[at, :] = times_tile(z0[at, :], old) + times_tile(z1[at, :], new)
+        z0[at, :] = times_tile(z0[at, :], first) - times_tile(w[at, :], second)
     stores = [pltpu.make_async_copy(z0, targets[0], store_sem.at[0])]
     stores[0].start()
-    for name in ("r1", "az", "p0"):
+    for name in ("b", "aw", "p0"):
         loads[name].wait()
     for plane in range(LOCAL_X):
         at = slice(32 * plane, 32 * plane + 32)
-        r1[at, :] = r1[at, :] - times_tile(az[at, :], new) - times_tile(p0[at, :], back)
-    stores.append(pltpu.make_async_copy(r1, targets[1], store_sem.at[1]))
+        b[at, :] = b[at, :] - times_tile(p0[at, :], first) + times_tile(aw[at, :], second)
+    stores.append(pltpu.make_async_copy(b, targets[1], store_sem.at[1]))
     stores[1].start()
     loads["sol"].wait()
     stores.append(pltpu.make_async_copy(sol, targets[2], store_sem.at[2]))
@@ -991,19 +1161,19 @@
     scratch = (
         [field] * 5
         + [rows(720), rows(720), rows(800), rows(800), rows(640)]
-        + [field] * 8
+        + [field] * 6
         + [rows(8)]
         + halo
         + halo
         + [rows(72), rows(8 * 63)]
         + [pltpu.SemaphoreType.DMA((count,)) for count in (48, 48, 63, 63, 6 + len(constants), len(OUT_NAMES))]
-        + [pltpu.VMEM(flags.shape, jnp.int32), pltpu.VMEM(coarse_row.shape, F32), rows(24)]
+        + [pltpu.VMEM(flags.shape, jnp.int32), pltpu.VMEM(coarse_row.shape, F32), rows(16)]
         + [pltpu.VMEM(table.shape, table.dtype) for table in constants]
     )
     return pl.pallas_call(
         functools.partial(body, sizes),
         out_shape=[
-            jax.ShapeDtypeStruct((24 if name == "steps" else ROWS, LOCAL_Z), F32) for name in OUT_NAMES
+            jax.ShapeDtypeStruct((16 if name == "steps" else ROWS, LOCAL_Z), F32) for name in OUT_NAMES
         ],
         in_specs=[far] * (6 + len(constants)),
         out_specs=[far] * len(OUT_NAMES),

time: 58.9 us -> 57.1 us (0.969)
  Pallas kernels: 58 us -> 56.3 us
    pallas_call x1, Pallas kernels: 55.8 us -> 54.1 us  [run_kernel(): pl.pallas_call(functools.partial(body, sizes), out_shape=[jax.ShapeDtypeS...]
where the time goes in v3:
time: 57.1 us; the launch traced here: 56.9 us
  Pallas kernels  56.3 us (99%)
  between operations  0.64 us (1%)
    pallas_call x1, Pallas kernels, run_kernel(): pl.pallas_call(functools.partial(body, sizes), out_shape=[jax.ShapeDtypeS...  54.1 us
    pallas_call x1, Pallas kernels, finish(): pl.pallas_call(finish_body, out_shape=[jax.ShapeDtypeStruct((ROWS, LOCAL_...  2.2 us

profile of v3, /device:TPU:1, one launch (start us, length us, event | category | flops | bytes accessed | tf_op | source)
XLA Modules:
  0.0 56.9 jit_solution(13007430489484964544)
XLA Ops:
  0.6 54.1 %shard_map.202 = (f32[512,128]{1,0:T(8,128)}, f32[512,128]{1,0:T(8,128)}, f32[512,128]{1,0:T(8,128)}, f32[512,128]{1,0:T(8,128)}, f32[512,128]{1,0:T(8,128)}, /*index=5*/f32[512,128]{1,0:T(8,128)}, f32[16,128]{1,0:T(8,128)}) custom-call(f32[512,128]{1,0:T(8,128)} %bitcast.7, f32[512,128]{1,0:T(8,128)} %bitcast.8, f32[512,128]{1,0:T(8,128)} %bitcast.9, ...), custom_call_target="tpu_custom_call" | custom-call | tf_op jit(solution)/shard_map/pallas_call | solution.py:1173
  54.7 2.2 %shard_map.203 = (f32[512,128]{1,0:T(8,128)}, f32[512,128]{1,0:T(8,128)}, f32[512,128]{1,0:T(8,128)}) custom-call(f32[512,128]{1,0:T(8,128)} %get-tuple-element.13.refs_0_, f32[512,128]{1,0:T(8,128)} %get-tuple-element.14.refs_1_, f32[512,128]{1,0:T(8,128)} %get-tuple-element.15.refs_2_, f32[512,128]{1,0:T(8,128)} %get-tuple-element.16.refs_3_, ...), custom_call_target="tpu_custom_call" | custom-call | tf_op jit(solution)/shard_map/pallas_call | solution.py:1141

commit v4 on v3

--- a/solution.py
+++ b/solution.py
@@ -430,12 +430,6 @@
         size = stage_sizes[stage]
         return sorted(range(1, size), key=lambda step: -min(step, size - step))
 
-    barrier = pltpu.get_barrier_semaphore()
-    partners = [neighbour(direction) for direction in DIRS]
-    for stage in range(3):
-        partners += [stage_partner(stage, step) for step in steps_of(stage)]
-    for partner in partners:
-        pl.semaphore_signal(barrier, inc=1, device_id=partner, device_id_type=MESH_ID)
     loads = {}
     wanted = [("rhs", rhs_h, buf["rhs"]), ("crow", crow_h, crow_ref)]
     wanted += [("sol", sol_h, buf["sol"]), ("kd", dif_h, buf["kd"]), ("flags", flags_h, flags_ref)]
@@ -443,6 +437,16 @@
     wanted += [("kc", coef_h, buf["kc"])]
     for at, (name, source, target) in enumerate(wanted):
         loads[name] = pltpu.make_async_copy(source, target, load_sem.at[at])
+    for name in ("rhs", "crow"):
+        loads[name].start()
+    barrier = pltpu.get_barrier_semaphore()
+    far = [(-min(step, stage_sizes[stage] - step), stage, step) for stage in (2, 1) for step in steps_of(stage)]
+    partners = [stage_partner(stage, step) for _, stage, step in sorted(far)]
+    partners += [neighbour(direction) for direction in DIRS]
+    partners += [stage_partner(0, step) for step in steps_of(0)]
+    for partner in partners:
+        pl.semaphore_signal(barrier, inc=1, device_id=partner, device_id_type=MESH_ID)
+    for name, _, _ in wanted[2:]:
         loads[name].start()
 
     row32 = lax.broadcasted_iota(jnp.int32, (32, 128), 0)
@@ -1087,16 +1091,6 @@
             values = values * x_hi
         buf["rhs"][at, :] = values
     store("aw", buf["rhs"])
-    total = jnp.broadcast_to(total_of(g_rows(2, 2)), (8, 128))
-    b_w, p_w, w_curve = [read_scalar(total, at) for at in range(3)]
-    rz1 = alpha0 * (alpha0 * p_w - b_w)
-    cross1 = curve0 - alpha0 * p_w
-    curve1 = cross1 - alpha0 * (p_w - alpha0 * w_curve)
-    beta = rz1 / rz0
-    alpha1 = rz1 / (curve1 + beta * (2.0 * cross1 + beta * curve0))
-    steps_ref[0:8, :] = alpha0 + alpha1 * (1.0 + beta)
-    steps_ref[8:16, :] = alpha0 * alpha1
-    store("steps", steps_ref)
     for name in halo_copies:
         for copy in halo_copies[name]:
             copy.wait_send()
@@ -1104,6 +1098,18 @@
         copy.wait_send()
     for copy in stores:
         copy.wait()
+    inverse = 1.0 / rz0
+    total = jnp.broadcast_to(total_of(g_rows(2, 2)), (8, 128))
+    b_w, p_w, w_curve = [read_scalar(total, at) for at in range(3)]
+    rz1 = alpha0 * (alpha0 * p_w - b_w)
+    cross1 = curve0 - alpha0 * p_w
+    curve1 = cross1 - alpha0 * (p_w - alpha0 * w_curve)
+    beta = rz1 * inverse
+    alpha1 = rz1 / (curve1 + beta * (2.0 * cross1 + beta * curve0))
+    steps_ref[0:8, :] = alpha0 + alpha1 * (1.0 + beta)
+    steps_ref[8:16, :] = alpha0 * alpha1
+    store("steps", steps_ref)
+    stores[-1].wait()
 
 
 def finish_body(*refs):

time: 57.1 us -> 57 us (level)
  no operation moved by 1% of the time
where the time goes in v4:
time: 57 us; the launch traced here: 56.8 us
  Pallas kernels  56.2 us (99%)
  between operations  0.64 us (1%)
    pallas_call x1, Pallas kernels, run_kernel(): pl.pallas_call(functools.partial(body, sizes), out_shape=[jax.ShapeDtypeS...  54 us
    pallas_call x1, Pallas kernels, finish(): pl.pallas_call(finish_body, out_shape=[jax.ShapeDtypeStruct((ROWS, LOCAL_...  2.2 us

profile of v4, /device:TPU:1, one launch (start us, length us, event | category | flops | bytes accessed | tf_op | source)
XLA Modules:
  0.0 56.8 jit_solution(393862708204006495)
XLA Ops:
  0.6 54.0 %shard_map.202 = (f32[512,128]{1,0:T(8,128)}, f32[512,128]{1,0:T(8,128)}, f32[512,128]{1,0:T(8,128)}, f32[512,128]{1,0:T(8,128)}, f32[512,128]{1,0:T(8,128)}, /*index=5*/f32[512,128]{1,0:T(8,128)}, f32[16,128]{1,0:T(8,128)}) custom-call(f32[512,128]{1,0:T(8,128)} %bitcast.7, f32[512,128]{1,0:T(8,128)} %bitcast.8, f32[512,128]{1,0:T(8,128)} %bitcast.9, ...), custom_call_target="tpu_custom_call" | custom-call | tf_op jit(solution)/shard_map/pallas_call | solution.py:1179
  54.6 2.2 %shard_map.203 = (f32[512,128]{1,0:T(8,128)}, f32[512,128]{1,0:T(8,128)}, f32[512,128]{1,0:T(8,128)}) custom-call(f32[512,128]{1,0:T(8,128)} %get-tuple-element.13.refs_0_, f32[512,128]{1,0:T(8,128)} %get-tuple-element.14.refs_1_, f32[512,128]{1,0:T(8,128)} %get-tuple-element.15.refs_2_, f32[512,128]{1,0:T(8,128)} %get-tuple-element.16.refs_3_, ...), custom_call_target="tpu_custom_call" | custom-call | tf_op jit(solution)/shard_map/pallas_call | solution.py:1147

commit v5 on v4

--- a/solution.py
+++ b/solution.py
@@ -403,7 +403,8 @@
     recv_bufs = dict(zip([r[0] for r in ROUNDS], refs[6:12]))
     g_send, g_recv, halo_send_sem, halo_recv_sem, g_send_sem, g_recv_sem = refs[12:18]
     load_sem, store_sem, flags_ref, crow_ref, steps_ref = refs[18:23]
-    tab = dict(zip(TABLE_NAMES, refs[23:]))
+    wide_recv, wide_send_sem, wide_recv_sem = refs[23:26]
+    tab = dict(zip(TABLE_NAMES, refs[26:]))
 
     grp = lax.axis_index("grp")
     dev = lax.axis_index("dev")
@@ -652,6 +653,56 @@
             middle = middle + jnp.where(tile_row == source, one, 0.0)
             scalars = two if scalars is None else scalars + two
         return (sides + pltpu.roll(middle, 64, 1), scalars)
+
+    wide_steps = [(j, k) for j in range(n_grp) for k in range(n_high) if j or k]
+    wide_steps.sort(key=lambda t: -min(t[0], n_grp - t[0]) - min(t[1], n_high - t[1]))
+
+    def wide_start(which):
+        row = total_of(g_rows(which, 0))
+        slot = 3 * which + 1
+        place = 64 * (which - 1) + high * 8 + grp
+        g_send[8 * slot : 8 * slot + 1, :] = row
+        wide_recv[pl.ds(place, 1), :] = row
+        for j, k in wide_steps:
+            pltpu.make_async_remote_copy(
+                src_ref=g_send.at[pl.ds(8 * slot, 1)],
+                dst_ref=wide_recv.at[pl.ds(place, 1)],
+                send_sem=wide_send_sem.at[which - 1],
+                recv_sem=wide_recv_sem.at[which - 1],
+                device_id=(
+                    (grp + j) & (n_grp - 1),
+                    ((high + k) & (n_high - 1)) * n_low + low,
+                ),
+                device_id_type=MESH_ID,
+            ).start()
+
+    def wide_wait(which, sem):
+        rows = wide_recv.at[pl.ds(64 * (which - 1), len(wide_steps))]
+        pltpu.make_async_copy(rows, rows, sem.at[which - 1]).wait()
+
+    def wide_tiles(which):
+        wide_wait(which, wide_recv_sem)
+        tiles = []
+        for at in range(n_high):
+            start = 64 * (which - 1) + 8 * at
+            tiles.append(jnp.where(tile_row < n_grp, wide_recv[start : start + 8, :], 0.0))
+        return tiles
+
+    def row_sum(tiles):
+        return jnp.broadcast_to(jnp.sum(weighted([1.0] * len(tiles), tiles), axis=0, keepdims=True), (8, 128))
+
+    def wide_finish(which):
+        tiles = wide_tiles(which)
+        parts = []
+        for part in range(3):
+            total = jnp.zeros((8, 128), F32)
+            for at, tile in enumerate(tiles):
+                first = n_low * at - 1
+                moved = pltpu.roll(tile, (first - reach * part + 256) % 128, 1)
+                inside = (tile_lane >= first) & (tile_lane < first + reach)
+                total = total + jnp.where(inside, moved, 0.0)
+            parts.append(total)
+        return (pltpu.roll(parts[0], 7, 0) + parts[1] + pltpu.roll(parts[2], 1, 0), row_sum(tiles))
 
     def read_scalar(tile, at):
         lanes = jnp.sum(jnp.where(tile_lane == at, tile, 0.0), axis=1, keepdims=True)
@@ -1048,12 +1099,11 @@
         buf["solraw"][at, :] = z_assembled(buf["solraw"][at, :])
     store("sol", buf["solraw"])
 
-    g_second(1)
+    wide_start(1)
     arrived("sti0")
     build_pin("sti0", buf["a1"])
     schwarz(buf["w"])
     exchange("sch1", buf["w"])
-    g_third(1)
     for plane in range(16):
         buf["p0"][32 * plane : 32 * plane + 32, :] = assembled_own(plane)
     add_arrived("sch1", buf["w"])
@@ -1061,7 +1111,7 @@
     sums = coarse_sums(buf["rhs"])
     b_w = product_of(buf["b"], buf["w"])
     p_w = product_of(buf["p0"], buf["w"])
-    total, scalars = g_finish(1)
+    total, scalars = wide_finish(1)
     coarse = coarse_values(total)
     image = coarse_image(energies, coarse)
     b_w = b_w + paired(coarse, right_sums)
@@ -1071,17 +1121,16 @@
     for at, value in enumerate((b_w, p_w, w_curve)):
         tile = jnp.where(tile_lane == at, value, tile)
     g_send_rows(2, 0, tile[0:1])
-    rz0 = read_scalar(scalars, 64)
-    curve0 = read_scalar(scalars, 65)
+    rz0 = read_scalar(scalars, 32)
+    curve0 = read_scalar(scalars, 33)
     alpha0 = rz0 / curve0
     add_coarse(buf["w"], coarse)
     stiff(buf["w"], buf["kc"], buf["rhs"])
     exchange("sti1", buf["rhs"])
     for name in ("z0", "w", "b", "p0"):
         store(name, buf[name])
-    g_send_rows(2, 1, total_of(g_rows(2, 0)))
+    wide_start(2)
     add_arrived("sti1", buf["rhs"])
-    g_send_rows(2, 2, total_of(g_rows(2, 1)))
     for plane in range(16):
         at = slice(32 * plane, 32 * plane + 32)
         values = z_assembled(buf["rhs"][at, :]) * keep_z * edge_y
@@ -1099,7 +1148,9 @@
     for copy in stores:
         copy.wait()
     inverse = 1.0 / rz0
-    total = jnp.broadcast_to(total_of(g_rows(2, 2)), (8, 128))
+    for which in (1, 2):
+        wide_wait(which, wide_send_sem)
+    total = row_sum(wide_tiles(2))
     b_w, p_w, w_curve = [read_scalar(total, at) for at in range(3)]
     rz1 = alpha0 * (alpha0 * p_w - b_w)
     cross1 = curve0 - alpha0 * p_w
@@ -1174,6 +1225,7 @@
         + [rows(72), rows(8 * 63)]
         + [pltpu.SemaphoreType.DMA((count,)) for count in (48, 48, 63, 63, 6 + len(constants), len(OUT_NAMES))]
         + [pltpu.VMEM(flags.shape, jnp.int32), pltpu.VMEM(coarse_row.shape, F32), rows(16)]
+        + [rows(128), pltpu.SemaphoreType.DMA((2,)), pltpu.SemaphoreType.DMA((2,))]
         + [pltpu.VMEM(table.shape, table.dtype) for table in constants]
     )
     return pl.pallas_call(

time: 57 us -> 54.6 us (0.958); the launches traced: 56.8 us -> 53.7 us
  Pallas kernels: 56.2 us -> 53 us
    pallas_call x1, Pallas kernels: 54 us -> 50.8 us  [run_kernel(): pl.pallas_call(functools.partial(body, sizes), out_shape=[jax.ShapeDtypeS...]
where the time goes in v5:
time: 54.6 us; the launch traced here: 53.7 us
  Pallas kernels  53 us (97%)
  between operations  0.64 us (1%)
    pallas_call x1, Pallas kernels, run_kernel(): pl.pallas_call(functools.partial(body, sizes), out_shape=[jax.ShapeDtypeS...  50.8 us
    pallas_call x1, Pallas kernels, finish(): pl.pallas_call(finish_body, out_shape=[jax.ShapeDtypeStruct((ROWS, LOCAL_...  2.2 us

profile of v5, /device:TPU:1, one launch (start us, length us, event | category | flops | bytes accessed | tf_op | source)
XLA Modules:
  0.0 53.7 jit_solution(3778301057101400833)
XLA Ops:
  0.6 50.8 %shard_map.202 = (f32[512,128]{1,0:T(8,128)}, f32[512,128]{1,0:T(8,128)}, f32[512,128]{1,0:T(8,128)}, f32[512,128]{1,0:T(8,128)}, f32[512,128]{1,0:T(8,128)}, /*index=5*/f32[512,128]{1,0:T(8,128)}, f32[16,128]{1,0:T(8,128)}) custom-call(f32[512,128]{1,0:T(8,128)} %bitcast.7, f32[512,128]{1,0:T(8,128)} %bitcast.8, f32[512,128]{1,0:T(8,128)} %bitcast.9, ...), custom_call_target="tpu_custom_call" | custom-call | tf_op jit(solution)/shard_map/pallas_call | solution.py:1231
  51.5 2.2 %shard_map.203 = (f32[512,128]{1,0:T(8,128)}, f32[512,128]{1,0:T(8,128)}, f32[512,128]{1,0:T(8,128)}) custom-call(f32[512,128]{1,0:T(8,128)} %get-tuple-element.13.refs_0_, f32[512,128]{1,0:T(8,128)} %get-tuple-element.14.refs_1_, f32[512,128]{1,0:T(8,128)} %get-tuple-element.15.refs_2_, f32[512,128]{1,0:T(8,128)} %get-tuple-element.16.refs_3_, ...), custom_call_target="tpu_custom_call" | custom-call | tf_op jit(solution)/shard_map/pallas_call | solution.py:1198
